TPU v7x, 512 devices: a whole 4x8x8 slice. The times are simulated.
512 devices in a mesh: dp: 64 (over y, z), tensor: 8 (over x, core).
Axes of the slice: x: 4, y: 8, z: 8, core: 2. Of those that a mesh axis runs over, the one named last changes fastest.
Arguments:
- activations: bfloat16 [65536, 3072], P('dp', 'tensor'), may hold values from -6 to 6
- out_grads: bfloat16 [65536, 2560], P('dp'), may hold values from -0.25 to 0.25
- residue: bfloat16 [64, 3072, 2560], P('dp', 'tensor'), may hold values from -6 to 6
- warm_start: bfloat16 [2560, 64], replicated, may hold values from -6 to 6
Outputs:
- update: bfloat16 [3072, 2560], P('tensor')
All inputs are finite; a program needn't handle non-finite values.
Results may differ from a plain program's by a relative error of at most 0.0011.
Values sent between devices are 32-bit elements; how exact they have to be, the bound alone decides.
No kernel may reach another device: no remote copies, remote signals or barrier semaphores. Data moves between devices by JAX's collectives and lax.ppermute only.
A program may use at most 64 MiB of HBM per device.

v0:
```python
import jax
import jax.numpy as jnp
from jax import lax
from jax.sharding import PartitionSpec as P

highest_precision = lax.Precision.HIGHEST
first_dims = (((0,), (0,)), ((), ()))


def whiten(lower_factor, matrix):
    return jax.scipy.linalg.solve_triangular(lower_factor, matrix.T, lower=True).T


def local(activations, out_grads, residue, warm_start):
    gradient = lax.dot_general(
        activations, out_grads, first_dims, preferred_element_type=jnp.float32
    )
    merged = gradient + residue[0].astype(jnp.float32)
    start_basis = warm_start.astype(jnp.float32)
    p_part = jnp.dot(merged, start_basis, precision=highest_precision)
    p_raw = lax.psum(p_part, "dp")
    gram_part = jnp.dot(p_raw.T, p_raw, precision=highest_precision)
    gram_matrix = lax.psum(gram_part, "tensor")
    lower_factor = jnp.linalg.cholesky(gram_matrix)
    p_orth = whiten(lower_factor, p_raw)
    q_part = lax.dot_general(merged, p_orth, first_dims, precision=highest_precision)
    factor = lax.psum(q_part, ("dp", "tensor"))
    return jnp.dot(p_orth, factor.T, precision=highest_precision).astype(jnp.bfloat16)


def solution(mesh):
    in_specs = (P("dp", "tensor"), P("dp", None), P("dp", "tensor", None), P())
    out_specs = P("tensor", None)
    return jax.shard_map(local, mesh=mesh, in_specs=in_specs, out_specs=out_specs, check_vma=False)
```

profile of v0, /device:TPU:1, one launch (start us, length us, event | category | flops | bytes accessed | tf_op | source)
XLA Modules:
  0.0 502.8 jit_solution(12040766350534882545)
XLA Ops:
  6.5 0.0 copy-start
  6.5 0.0 copy-start.2
  6.5 0.0 all-reduce.3.cloned.1.call-start
  6.5 1.1 copy-done
  7.7 5.4 %convolution_add_fusion = f32[384,2560]{1,0:T(8,128)S(1)} fusion(bf16[1024,384]{1,0:T(8,128)(2,1)S(1)} %copy-done, bf16[1024,2560]{1,0:T(8,128)(2,1)} %param.5, bf16[1,384,2560]{2,1,0:T(8,128)(2,1)} %param.6), kind=kOutput, calls=%fused_computation | convolution fusion | flops 2015232000 | bytes 11927552 | tf_op jit(solution)/shard_map/dot_general | solution.py:15
  13.1 0.0 copy-start.1
  13.1 1.9 copy-done.1
  15.0 0.0 copy-done.2
  15.0 2.8 fusion.4
  17.8 0.0 all-reduce.3.cloned.1.call-update
  17.8 0.0 all-reduce.5.cloned.1.call-start
  17.9 151.9 %all-reduce.3.cloned.1.call-done = f32[384,64]{0,1:T(8,128)} async-done(((f32[384,64]{0,1:T(8,128)}), f32[384,64]{0,1:T(8,128)}) %all-reduce.3.cloned.1.call-update) | async-done | bytes 98320 | tf_op jit(solution)/shard_map/psum | solution.py:21
  169.8 1.2 fusion.5
  171.0 24.6 %psum.22 = f32[64,64]{0,1:T(8,128)S(1)} all-reduce(f32[64,64]{0,1:T(8,128)S(1)} %fusion.5), channel_id=1, replica_groups=mesh['dp'=64,'tensor'=8] {'tensor'}, use_global_device_ids=true, to_apply=%region_1.0 | all-reduce | flops 4096 | bytes 32768 | tf_op jit(solution)/shard_map/psum | solution.py:23
  195.6 0.1 copy.6
  195.7 5.8 %cholesky.16 = f32[64,64]{1,0:T(8,128)S(1)} custom-call(f32[64,64]{1,0:T(8,128)S(1)} %fusion.3), custom_call_target="Cholesky" | custom-call | tf_op jit(solution)/shard_map/jit(cholesky)/cholesky | solution.py:24
  201.6 0.6 compare_reduce_fusion
  202.2 0.7 fusion
  202.9 4.9 custom-call.7
  207.8 1.2 fusion.1
  209.0 9.5 %fusion.6 = f32[2560,64]{1,0:T(8,128)} fusion(f32[384,2560]{1,0:T(8,128)} %copy-done.1, f32[64,384]{1,0:T(8,128)S(1)} %fusion.1), kind=kOutput, calls=%fused_computation.14 | convolution fusion | flops 754974720 | bytes 4685824 | tf_op jit(solution)/shard_map/dot_general | solution.py:26
  218.5 0.0 all-reduce.5.cloned.1.call-update
  218.6 271.5 %all-reduce.5.cloned.1.call-done = f32[2560,64]{1,0:T(8,128)} async-done(((f32[2560,64]{1,0:T(8,128)}), f32[2560,64]{1,0:T(8,128)}) %all-reduce.5.cloned.1.call-update) | async-done | bytes 655376 | tf_op jit(solution)/shard_map/psum | solution.py:27
  490.1 5.9 %convolution_convert_fusion = bf16[384,2560]{1,0:T(8,128)(2,1)} fusion(f32[64,384]{1,0:T(8,128)S(1)} %fusion.1, f32[2560,64]{1,0:T(8,128)} %all-reduce.5.cloned.1.call-done), kind=kOutput, calls=%fused_computation.1 | convolution fusion | flops 755957760 | bytes 2719744 | tf_op jit(solution)/shard_map/dot_general | solution.py:28
  (2 shorter events, 0.0 us)
Async XLA Ops:
  6.5 1.1 copy-start
  6.5 8.4 %copy-start.2 = (bf16[2560,64]{0,1:T(8,128)(2,1)S(1)}, bf16[2560,64]{0,1:T(8,128)(2,1)}, u32[]{:S(2)}) copy-start(bf16[2560,64]{0,1:T(8,128)(2,1)} %param.7) | copy-start | bytes 983044
  6.5 163.3 %all-reduce.3.cloned.1.call-start = ((), (), s32[]{:S(2)}) async-start(), calls=%async_computation | async-start | bytes 196608 | tf_op jit(solution)/shard_map/psum | solution.py:21
  13.1 1.9 copy-start.1
  17.8 472.3 %all-reduce.5.cloned.1.call-start = ((), (), s32[]{:S(2)}) async-start(), calls=%async_computation.1 | async-start | bytes 2621440 | tf_op jit(solution)/shard_map/psum | solution.py:27
Sparse Core Ops, SparseCore 0:
  17.9 151.8 all-reduce.2
  218.7 271.3 all-reduce.4
where the time goes:
time: 504 us; the launch traced here: 503 us
  waiting for transfers between devices  424 us (84%)
  matrix products  26.1 us (5%)
  blocking collectives  24.6 us (5%)
  between operations  13.5 us (3%)
  other arithmetic  12.1 us (2%)
    psum x1, waiting for transfers between devices, local(): factor = lax.psum(q_part, ('dp', 'tensor'))  272 us
    psum x1, waiting for transfers between devices, local(): p_raw = lax.psum(p_part, 'dp')  152 us
    psum x1, blocking collectives, local(): gram_matrix = lax.psum(gram_part, 'tensor')  24.6 us
  transfers between devices with their start and end apart: 2, of which 2 were waited for; matrix products, arithmetic and copies ran while one was open for 0% of the time, Pallas kernels for 0%

commit v1 on v0

v1 whole, which is shorter than its diff:
```python
import math

import jax
import jax.numpy as jnp
from jax import lax
from jax.sharding import Mesh, PartitionSpec as P

RANK = 64
GRID = {"y": 8, "z": 8, "x": 4, "core": 2}
highest_precision = lax.Precision.HIGHEST
first_dims = (((0,), (0,)), ((), ()))
last_dims = (((1,), (1,)), ((), ()))


def dot32(left, right, dims=(((1,), (0,)), ((), ()))):
    return lax.dot_general(left, right, dims, preferred_element_type=jnp.float32)


def split(value, terms):
    parts = []
    for _ in range(terms):
        part = lax.reduce_precision(value, 8, 7)
        parts.append(part.astype(jnp.bfloat16))
        value = value - part
    return parts


def peers_of(axes):
    return math.prod(GRID[axis] for axis in axes)


def scatter_sum(value, axes):
    peers = peers_of(axes)
    chunks = value.reshape(peers, value.shape[0] // peers, value.shape[1])
    return jnp.sum(lax.all_to_all(chunks, axes, 0, 0), axis=0)


def spread(value, axes):
    copies = jnp.broadcast_to(value[None], (peers_of(axes), *value.shape))
    return lax.all_to_all(copies, axes, 0, 0)


def gather(value, axes):
    peers = peers_of(axes)
    return spread(value, axes).reshape(peers * value.shape[0], value.shape[1])


def local(activations, out_grads, residue, warm_start):
    residue = residue[0]
    projected = jnp.concatenate(split(dot32(out_grads, warm_start), 3), axis=1)
    terms = dot32(projected, activations, first_dims)
    left = terms[:RANK] + terms[RANK : 2 * RANK] + terms[2 * RANK :]
    left = left + dot32(warm_start, residue, (((0,), (1,)), ((), ())))
    left = scatter_sum(left, ("z",))
    left = jnp.sum(spread(left, ("y",)), axis=0)
    left = gather(left, ("z",))

    merged = dot32(activations, out_grads, first_dims) + residue.astype(jnp.float32)
    high, low = split(merged, 2)
    left_high, left_low = split(left, 2)
    right = dot32(left_high, high) + (dot32(left_low, high) + dot32(left_high, low))
    share = 1.0 / (GRID["y"] * GRID["z"])
    gram = lax.dot_general(left * share, left, last_dims, precision=highest_precision)
    both = jnp.concatenate([right, gram], axis=1)
    both = scatter_sum(both, ("core",))
    both = scatter_sum(both, ("z", "x"))
    both = jnp.sum(spread(both, ("y",)), axis=0)
    both = gather(both, ("z", "x"))
    both = lax.all_gather(both, "core", axis=0, tiled=True)
    right, gram = both[:, :-RANK], both[:, -RANK:]

    lower_factor = jnp.linalg.cholesky(gram)
    inverse = jax.scipy.linalg.solve_triangular(lower_factor, jnp.eye(RANK, dtype=jnp.float32), lower=True)
    whiten = lax.dot_general(inverse, inverse, first_dims, precision=highest_precision)
    scaled = lax.dot_general(left, whiten, first_dims, precision=highest_precision)
    scaled_high, scaled_low = split(scaled, 2)
    right_high, right_low = split(right, 2)
    update = dot32(
        jnp.concatenate([scaled_high, scaled_high, scaled_low], axis=1),
        jnp.concatenate([right_high, right_low, right_high], axis=0),
    )
    return update.astype(jnp.bfloat16)


def solution(mesh):
    fine = Mesh(mesh.devices.reshape(*GRID.values()), tuple(GRID))
    dp, tensor = ("y", "z"), ("x", "core")
    in_specs = (P(dp, tensor), P(dp, None), P(dp, tensor, None), P())
    return jax.shard_map(local, mesh=fine, in_specs=in_specs, out_specs=P(tensor, None), check_vma=False)
```

time: 504 us -> 136 us (0.27)
  waiting for transfers between devices: 424 us -> 0.88 us
  blocking collectives: 24.6 us -> 93.7 us
  between operations: 13.5 us -> 0.21 us
  matrix products: 26.1 us -> 20.6 us
    psum x2 -> x0, waiting for transfers between devices: 423 us -> none  [the longest x1 272 us: local(): factor = lax.psum(q_part, ('dp', 'tensor'))]
    all_to_all x0 -> x6, blocking collectives: none -> 86.9 us  [the longest x3 47.4 us: scatter_sum(): return jnp.sum(lax.all_to_all(chunks, axes, 0, 0), axis=0)]
    psum x1 -> x0, blocking collectives: 24.6 us -> none  [local(): gram_matrix = lax.psum(gram_part, 'tensor')]
    all_gather x0 -> x1, blocking collectives: none -> 6.74 us  [local(): both = lax.all_gather(both, 'core', axis=0, tiled=True)]
    dot_general x5 -> x11, matrix products: 24.9 us -> 20.4 us  [the longest x8 19.6 us: dot32(): lax.dot_general(left, right, dims, preferred_element_type=jnp.float32)]
  transfers between devices with their start and end apart: 2 -> 1, of which waited for: 2 -> 1; matrix products, arithmetic and copies ran while one was open for 0% -> 5% of each run, Pallas kernels for 0% -> 0%
where the time goes in v1:
time: 136 us; the launch traced here: 135 us
  blocking collectives  93.7 us (69%)
  matrix products  20.6 us (15%)
  other arithmetic  13.5 us (10%)
  starting transfers between devices  3.36 us (2%)
  local copies, waits for them, and re-layouts  3.03 us (2%)
    all_to_all x3, blocking collectives, scatter_sum(): return jnp.sum(lax.all_to_all(chunks, axes, 0, 0), axis=0)  47.4 us
    all_to_all x3, blocking collectives, spread(): return lax.all_to_all(copies, axes, 0, 0)  39.6 us
    dot_general x8, matrix products, dot32(): lax.dot_general(left, right, dims, preferred_element_type=jnp.float32)  19.6 us
    all_gather x1, blocking collectives, local(): both = lax.all_gather(both, 'core', axis=0, tiled=True)  6.74 us
    another operation x3, other arithmetic, local(): lower_factor = jnp.linalg.cholesky(gram)  6.52 us
    another operation x2, other arithmetic, local(): jax.scipy.linalg.solve_triangular(lower_factor, jnp.eye(RANK, dtype=jnp.f...  5.55 us
    all_to_all x1, starting transfers between devices, spread(): return lax.all_to_all(copies, axes, 0, 0)  3.36 us
  transfers between devices with their start and end apart: 1, of which 1 were waited for; matrix products, arithmetic and copies ran while one was open for 5% of the time, Pallas kernels for 0%

profile of v1, /device:TPU:1, one launch (start us, length us, event | category | flops | bytes accessed | tf_op | source)
XLA Modules:
  0.0 135.3 jit_solution(9364490116799065180)
XLA Ops:
  0.0 4.4 %reduce-precision_convert_fusion.5 = (bf16[1024,64]{0,1:T(8,128)(2,1)S(1)}, bf16[1024,64]{0,1:T(8,128)(2,1)S(1)}, bf16[1024,64]{0,1:T(8,128)(2,1)S(1)}) fusion(bf16[1024,2560]{1,0:T(8,128)(2,1)} %param.5, bf16[2560,64]{0,1:T(8,128)(2,1)} %param.7), kind=kOutput, calls=%fused_computation.32 | convolution fusion | flops 336068608 | bytes 5963776 | tf_op jit(solution)/shard_map/dot_general | solution.py:16
  4.4 0.4 fusion.19
  4.8 0.8 fusion.15
  5.6 18.3 %all_to_all.35 = f32[8,8,384]{2,1,0:T(8,128)S(1)} all-to-all(f32[8,8,384]{2,1,0:T(8,128)S(1)} %fusion.15), channel_id=1, replica_groups=mesh['y'=8,'z'=8,'x'=4,'core'=2] {'z'}, dimensions={0} | all-to-all | bytes 196608 | tf_op jit(solution)/shard_map/all_to_all | solution.py:35
  23.9 14.2 %all_to_all.36 = f32[8,8,384]{2,1,0:T(8,128)S(1)} all-to-all(f32[8,8,384]{2,1,0:T(8,128)S(1)} %broadcast_in_dim.9), channel_id=1, replica_groups=mesh['y'=8,'z'=8,'x'=4,'core'=2] {'y'}, dimensions={0} | all-to-all | bytes 196608 | tf_op jit(solution)/shard_map/all_to_all | solution.py:40
  38.1 0.6 broadcast_in_dim.10
  38.7 3.4 %all-to-all-start.2 = ((f32[8,8,384]{2,1,0:T(8,128)}), f32[8,8,384]{2,1,0:T(8,128)S(1)}, u32[]{:S(2)}, u32[]{:S(2)}) async-start(f32[8,8,384]{2,1,0:T(8,128)} %broadcast_in_dim.10), calls=%async_computation.2 | async-start | bytes 196608 | tf_op jit(solution)/shard_map/all_to_all | solution.py:40
  42.1 6.6 %convolution_add_fusion = f32[384,2560]{1,0:T(8,128)} fusion(bf16[1024,384]{1,0:T(8,128)(2,1)S(1)} %copy-done, bf16[1024,2560]{1,0:T(8,128)(2,1)} %param.5, bf16[1,384,2560]{2,1,0:T(8,128)(2,1)S(1)} %copy-done.2), kind=kOutput, calls=%fused_computation.2 | convolution fusion | flops 2015232000 | bytes 11927552 | tf_op jit(solution)/shard_map/dot_general | solution.py:16
  48.7 0.9 all-to-all-done.2
  49.6 0.2 fusion.36
  49.9 2.7 %fusion.18 = f32[64,2560]{1,0:T(8,128)S(1)} fusion(f32[384,2560]{1,0:T(8,128)} %convolution_add_fusion, f32[8,8,384]{2,1,0:T(8,128)S(1)} %all-to-all-done.2), kind=kOutput, calls=%fused_computation.21 | convolution fusion | flops 127893504 | bytes 4685824 | tf_op jit(solution)/shard_map/dot_general | solution.py:16
  52.6 0.3 copy-done.1
  52.9 0.6 convolution_add_fusion.1
  53.5 0.5 convolution_add_fusion.2
  54.0 8.6 %all_to_all.37 = f32[2,32,2624]{2,1,0:T(8,128)S(1)} all-to-all(f32[2,32,2624]{2,1,0:T(8,128)S(1)} %bitcast.48), channel_id=1, replica_groups=mesh['y'=8,'z'=8,'x'=4,'core'=2] {'core'}, dimensions={0} | all-to-all | bytes 1343488 | tf_op jit(solution)/shard_map/all_to_all | solution.py:35
  62.6 0.2 reshape.41
  62.9 20.5 %all_to_all.38 = f32[32,1,2624]{2,1,0:T(1,128)S(1)} all-to-all(f32[32,1,2624]{2,1,0:T(1,128)S(1)} %reshape.41), channel_id=1, replica_groups=mesh['y'=8,'z'=8,'x'=4,'core'=2] {'z','x'}, dimensions={0} | all-to-all | bytes 671744 | tf_op jit(solution)/shard_map/all_to_all | solution.py:35
  83.4 0.2 reduce_sum.48
  83.6 9.8 %all_to_all.39 = f32[8,1,2624]{2,1,0:T(1,128)S(1)} all-to-all(f32[8,1,2624]{2,1,0:T(1,128)S(1)} %broadcast_in_dim.11), channel_id=1, replica_groups=mesh['y'=8,'z'=8,'x'=4,'core'=2] {'y'}, dimensions={0} | all-to-all | bytes 167936 | tf_op jit(solution)/shard_map/all_to_all | solution.py:40
  93.5 0.2 broadcast_in_dim.12
  93.7 15.5 %all_to_all.40 = f32[32,1,2624]{2,1,0:T(1,128)S(1)} all-to-all(f32[32,1,2624]{2,1,0:T(1,128)S(1)} %broadcast_in_dim.12), channel_id=1, replica_groups=mesh['y'=8,'z'=8,'x'=4,'core'=2] {'z','x'}, dimensions={0} | all-to-all | bytes 671744 | tf_op jit(solution)/shard_map/all_to_all | solution.py:40
  109.3 6.7 %all-gather = f32[64,1,2624]{2,1,0:T(1,128)S(1)} all-gather(f32[32,1,2624]{2,1,0:T(1,128)S(1)} %all_to_all.40), channel_id=2, replica_groups=mesh['y'=8,'z'=8,'x'=4,'core'=2] {'core'}, dimensions={0}, use_global_device_ids=true | all-gather | bytes 1007616 | tf_op jit(solution)/shard_map/all_gather | solution.py:69
  116.0 1.5 %copy.11 = f32[64,1,2624]{0,2,1:T(8,128)S(1)} copy(f32[64,1,2624]{2,1,0:T(1,128)S(1)} %all-gather) | data formatting | bytes 1343488 | tf_op jit(solution)/shard_map/all_gather | solution.py:69
  117.5 1.0 fusion.6
  118.7 5.8 %cholesky.17 = f32[64,64]{1,0:T(8,128)S(1)} custom-call(f32[64,64]{1,0:T(8,128)S(1)} %fusion.47), custom_call_target="Cholesky" | custom-call | tf_op jit(solution)/shard_map/jit(cholesky)/cholesky | solution.py:72
  124.6 0.6 compare_reduce_fusion
  125.2 0.7 fusion.44
  125.9 4.9 %custom-call.7 = f32[1,64,64]{1,2,0:T(8,128)S(1)} custom-call(f32[1,64,64]{2,1,0:T(8,128)S(1)} %fusion.44), custom_call_target="InvertDiagBlocksLowerTriangular" | custom-call | tf_op jit(solution)/shard_map/jit(_solve_triangular)/triangular_solve | solution.py:73
  130.8 0.2 fusion.45
  131.0 0.2 fusion.51
  131.2 0.3 reduce-precision_convert_fusion.6
  131.5 3.7 %convolution_convert_fusion = bf16[384,2560]{1,0:T(8,128)(2,1)} fusion(bf16[64,2560]{0,1:T(8,128)(2,1)} %get-tuple-element.6, bf16[64,2560]{0,1:T(8,128)(2,1)S(1)} %get-tuple-element.5, bf16[384,64]{0,1:T(8,128)(2,1)S(1)} %get-tuple-element.11, bf16[384,64]{0,1:T(8,128)(2,1)S(1)} %get-tuple-element.10), kind=kOutput, calls=%fused_computation.3 | convolution fusion | flops 381861888 | bytes 2719744 | tf_op jit(solution)/shard_map/dot_general | solution.py:16
  (18 shorter events, 0.4 us)
Async XLA Ops:
  0.0 4.4 %copy-start = (bf16[1024,384]{1,0:T(8,128)(2,1)S(1)}, bf16[1024,384]{1,0:T(8,128)(2,1)}, u32[]{:S(2)}) copy-start(bf16[1024,384]{1,0:T(8,128)(2,1)} %param.4) | copy-start | bytes 2359300
  0.0 4.8 %copy-start.3 = (bf16[2560,64]{0,1:T(8,128)(2,1)S(1)}, bf16[2560,64]{0,1:T(8,128)(2,1)}, u32[]{:S(2)}) copy-start(bf16[2560,64]{0,1:T(8,128)(2,1)} %param.7) | copy-start | bytes 983044
  0.0 4.8 %copy-start.2 = (bf16[1,384,2560]{2,1,0:T(8,128)(2,1)S(1)}, bf16[1,384,2560]{2,1,0:T(8,128)(2,1)}, u32[]{:S(2)}) copy-start(bf16[1,384,2560]{2,1,0:T(8,128)(2,1)} %param.6) | copy-start | bytes 5898244
  38.7 10.9 %all-to-all-start.2 = ((f32[8,8,384]{2,1,0:T(8,128)}), f32[8,8,384]{2,1,0:T(8,128)S(1)}, u32[]{:S(2)}, u32[]{:S(2)}) async-start(f32[8,8,384]{2,1,0:T(8,128)} %broadcast_in_dim.10), calls=%async_computation.2 | async-start | bytes 196608 | tf_op jit(solution)/shard_map/all_to_all | solution.py:40
  49.6 3.3 %copy-start.1 = (f32[384,2560]{1,0:T(8,128)S(1)}, f32[384,2560]{1,0:T(8,128)}, u32[]{:S(2)}) copy-start(f32[384,2560]{1,0:T(8,128)} %convolution_add_fusion) | copy-start | bytes 11796484

commit v2 on v0

v2 whole, which is shorter than its diff:
```python
import functools
import math

import jax
import jax.numpy as jnp
from jax import lax
from jax.experimental import pallas as pl
from jax.experimental.pallas import tpu as pltpu
from jax.sharding import Mesh, PartitionSpec as P

RANK = 64
HALF = RANK // 2
COL_BLOCK = 512
LEFT_STEPS = 4
PAIR = 2
LANES = 2 * RANK
GRAM = RANK * RANK // PAIR
GRID = {"yA": 2, "yB": 2, "yC": 2, "zA": 2, "zB": 2, "zC": 2, "x": 4, "core": 2}
DP = ("yA", "yB", "yC", "zA", "zB", "zC")
TENSOR = ("x", "core")
NEAR = ("yC", "zC")
NEAR_X = ("yC", "zC", "x")
FAR = ("yA", "yB", "zA", "zB")

highest_precision = lax.Precision.HIGHEST
plain_dims = (((1,), (0,)), ((), ()))
first_dims = (((0,), (0,)), ((), ()))
last_dims = (((1,), (1,)), ((), ()))


def dot32(left, right, dims=plain_dims):
    return lax.dot_general(left, right, dims, preferred_element_type=jnp.float32)


def dot_exact(left, right, dims=plain_dims):
    return lax.dot_general(
        left, right, dims, precision=highest_precision, preferred_element_type=jnp.float32
    )


def split(value, terms):
    parts = []
    for _ in range(terms):
        part = value.astype(jnp.bfloat16)
        parts.append(part)
        value = value - part.astype(jnp.float32)
    return parts


def params(megabytes):
    return pltpu.CompilerParams(vmem_limit_bytes=megabytes * 1024 * 1024)


def cost(flops, moved):
    return pl.CostEstimate(flops=flops, bytes_accessed=moved, transcendentals=0)


def left_kernel(act_ref, grad_ref, res_ref, warm_ref, out_ref, total, res_part):
    step = pl.program_id(0)
    warm = warm_ref[...]
    projected = jnp.concatenate(split(dot32(grad_ref[...], warm, last_dims), 3), axis=1)
    terms = dot32(projected, act_ref[...], first_dims)
    terms = terms[:RANK] + (terms[RANK : 2 * RANK] + terms[2 * RANK :])
    height = res_ref.shape[0]
    res_part[pl.ds(pl.multiple_of(step * height, 8), height), :] = dot32(res_ref[...], warm, last_dims)

    @pl.when(step == 0)
    def _():
        total[...] = terms

    @pl.when(step > 0)
    def _():
        total[...] += terms

    @pl.when(step == pl.num_programs(0) - 1)
    def _():
        out_ref[...] = total[...] + res_part[...].T


def left_product(activations, out_grads, residue, warm_start):
    tokens, rows = activations.shape
    cols = out_grads.shape[1]
    step_tokens, step_rows = tokens // LEFT_STEPS, rows // LEFT_STEPS
    return pl.pallas_call(
        left_kernel,
        grid=(LEFT_STEPS,),
        in_specs=[
            pl.BlockSpec((step_tokens, rows), lambda i: (i, 0)),
            pl.BlockSpec((step_tokens, cols), lambda i: (i, 0)),
            pl.BlockSpec((step_rows, cols), lambda i: (i, 0)),
            pl.BlockSpec((RANK, cols), lambda i: (0, 0)),
        ],
        out_specs=pl.BlockSpec((RANK, rows), lambda i: (0, 0)),
        out_shape=jax.ShapeDtypeStruct((RANK, rows), jnp.float32),
        scratch_shapes=[
            pltpu.VMEM((RANK, rows), jnp.float32),
            pltpu.VMEM((rows, RANK), jnp.float32),
        ],
        compiler_params=params(60),
        cost_estimate=cost(2 * tokens * cols * RANK, 2 * cols * (tokens + rows)),
    )(activations, out_grads, residue, warm_start.T)


def merged_kernel(act_ref, grad_ref, res_ref, high_ref, low_ref, act_t):
    @pl.when(pl.program_id(0) == 0)
    def _():
        act_t[...] = act_ref[...].T

    merged = dot32(act_t[...], grad_ref[...]) + res_ref[...].astype(jnp.float32)
    high_ref[...], low_ref[...] = split(merged, 2)


def merged_terms(activations, out_grads, residue):
    tokens, rows = activations.shape
    cols = out_grads.shape[1]
    block = pl.BlockSpec((rows, COL_BLOCK), lambda i: (0, i))
    return pl.pallas_call(
        merged_kernel,
        grid=(cols // COL_BLOCK,),
        in_specs=[
            pl.BlockSpec((tokens, rows), lambda i: (0, 0)),
            pl.BlockSpec((tokens, COL_BLOCK), lambda i: (0, i)),
            block,
        ],
        out_specs=[block, block],
        out_shape=[jax.ShapeDtypeStruct((rows, cols), jnp.bfloat16)] * 2,
        scratch_shapes=[pltpu.VMEM((rows, tokens), jnp.bfloat16)],
        compiler_params=params(36),
        cost_estimate=cost(2 * tokens * cols * rows, 2 * cols * (tokens + 3 * rows)),
    )(activations, out_grads, residue)


def right_kernel(half_ref, left_ref, high_ref, low_ref, out_ref, stacked):
    step = pl.program_id(0)
    cols = pl.num_programs(0) * COL_BLOCK

    @pl.when(step == 0)
    def _():
        start = pl.multiple_of(half_ref[0] * HALF, HALF)
        parts = split(left_ref[pl.ds(start, HALF), :], 2)
        stacked[...] = jnp.concatenate(parts, axis=0)
        left = left_ref[...]
        gram = dot_exact(left, left, last_dims)
        gram = jnp.concatenate([gram[:HALF], gram[HALF:]], axis=1)
        for i in range(HALF // PAIR):
            place = pl.ds(cols + i * LANES, LANES)
            piece = gram[i * PAIR : (i + 1) * PAIR, :]
            out_ref[:, :, place] = jnp.broadcast_to(piece[None], (HALF // PAIR, PAIR, LANES))

    both = dot32(stacked[...], high_ref[...])
    small = dot32(stacked[:HALF], low_ref[...])
    place = pl.ds(pl.multiple_of(step * COL_BLOCK, COL_BLOCK), COL_BLOCK)
    product = both[:HALF] + (both[HALF:] + small)
    out_ref[:, :, place] = product.reshape(HALF // PAIR, PAIR, COL_BLOCK)


def right_product(half, left, high, low):
    rows, cols = high.shape
    shape = (HALF // PAIR, PAIR, cols + GRAM)
    block = pl.BlockSpec((rows, COL_BLOCK), lambda i: (0, i))
    return pl.pallas_call(
        right_kernel,
        grid=(cols // COL_BLOCK,),
        in_specs=[
            pl.BlockSpec(memory_space=pltpu.SMEM),
            pl.BlockSpec((RANK, rows), lambda i: (0, 0)),
            block,
            block,
        ],
        out_specs=pl.BlockSpec(shape, lambda i: (0, 0, 0)),
        out_shape=jax.ShapeDtypeStruct(shape, jnp.float32),
        scratch_shapes=[pltpu.VMEM((2 * HALF, rows), jnp.bfloat16)],
        compiler_params=params(16),
        cost_estimate=cost(6 * rows * cols * HALF, 4 * cols * rows),
    )(half, left, high, low)


def whiten_kernel(copies, gram_ref, left_ref, out_ref):
    first = gram_ref.shape[1] - GRAM
    gram = jnp.concatenate(
        [gram_ref[:, first + i * LANES : first + (i + 1) * LANES] for i in range(HALF // PAIR)], axis=0
    )
    gram = jnp.concatenate([gram[:, :RANK], gram[:, RANK:]], axis=0) * (1.0 / copies)
    row = lax.broadcasted_iota(jnp.int32, (RANK, RANK), 0)
    col = lax.broadcasted_iota(jnp.int32, (RANK, RANK), 1)
    work = jnp.concatenate([gram, (row == col).astype(jnp.float32)], axis=1)
    tall = lax.broadcasted_iota(jnp.int32, (RANK, 2 * RANK), 0)
    for k in range(RANK - 1):
        pivot = work[k : k + 1, :]
        scale = work[:, k : k + 1] / pivot[:, k : k + 1]
        work = jnp.where(tall > k, work - scale * pivot, work)
    inverse = work[:, RANK:]
    diagonal = jnp.sum(jnp.where(row == col, work[:, :RANK], 0.0), axis=1, keepdims=True)
    basis = dot_exact(inverse, left_ref[...])
    scaled = dot_exact(basis, inverse / diagonal, first_dims)
    high, low = split(scaled, 2)
    out_ref[...] = jnp.concatenate([high, high, low], axis=1)


def whiten(right, left):
    rows = left.shape[1]
    return pl.pallas_call(
        functools.partial(whiten_kernel, peers_of(NEAR)),
        out_shape=jax.ShapeDtypeStruct((rows, 3 * RANK), jnp.bfloat16),
        compiler_params=params(16),
        cost_estimate=cost(400_000_000, 4_000_000),
    )(right, left)


def update_kernel(scaled_ref, right_ref, out_ref):
    right = right_ref[...].reshape(RANK, out_ref.shape[1])
    high, low = split(right, 2)
    terms = jnp.concatenate([high, low, high], axis=0)
    out_ref[...] = dot32(scaled_ref[...], terms).astype(jnp.bfloat16)


def update_product(scaled, right):
    rows, cols = scaled.shape[0], right.shape[-1]
    return pl.pallas_call(
        update_kernel,
        grid=(cols // COL_BLOCK,),
        in_specs=[
            pl.BlockSpec(scaled.shape, lambda i: (0, 0)),
            pl.BlockSpec((2, HALF // PAIR, PAIR, COL_BLOCK), lambda i: (0, 0, 0, i)),
        ],
        out_specs=pl.BlockSpec((rows, COL_BLOCK), lambda i: (0, i)),
        out_shape=jax.ShapeDtypeStruct((rows, cols), jnp.bfloat16),
        compiler_params=params(16),
        cost_estimate=cost(6 * rows * cols * RANK, 2 * cols * rows),
    )(scaled, right)


def peers_of(axes):
    return math.prod(GRID[axis] for axis in axes)


def scatter_sum(chunks, axes):
    return jnp.sum(lax.all_to_all(chunks, axes, 0, 0), axis=0)


def spread(value, axes):
    copies = jnp.broadcast_to(value[None], (peers_of(axes), *value.shape))
    return lax.all_to_all(copies, axes, 0, 0)


def after(first, *values):
    return lax.optimization_barrier((first, *values))


def local(activations, out_grads, residue, warm_start):
    residue = residue[0]
    left = left_product(activations, out_grads, residue, warm_start)
    left = scatter_sum(left.reshape(peers_of(NEAR), -1, left.shape[1]), NEAR)
    left, activations = after(left, activations)
    high, low = merged_terms(activations, out_grads, residue)
    left = jnp.sum(spread(left, FAR), axis=0)
    left, high, low = after(left, high, low)
    left = spread(left, NEAR).reshape(RANK, -1)

    core = lax.axis_index("core").astype(jnp.int32).reshape(1)
    sent = right_product(1 - core, left, high, low)
    kept = right_product(core, left, high, low)
    both = kept + lax.ppermute(sent, "core", [(0, 1), (1, 0)])
    right = scatter_sum(both, NEAR_X)
    scaled = whiten(right, left)
    right = jnp.sum(spread(right[:, : high.shape[1]], FAR), axis=0)
    right, scaled = after(right, scaled)
    right = lax.all_gather(spread(right, NEAR_X), "core", axis=0)
    return update_product(scaled, right)


def solution(mesh):
    fine = Mesh(mesh.devices.reshape(*GRID.values()), tuple(GRID))
    in_specs = (P(DP, TENSOR), P(DP, None), P(DP, TENSOR, None), P())
    return jax.shard_map(local, mesh=fine, in_specs=in_specs, out_specs=P(TENSOR, None), check_vma=False)
```

time: 504 us -> 124 us (0.25)
  waiting for transfers between devices: 424 us -> 18.1 us
  starting transfers between devices: 0.04 us -> 28.8 us
  matrix products: 26.1 us -> 0 us
  Pallas kernels: 0 us -> 25.5 us
  blocking collectives: 24.6 us -> 40.6 us
  between operations: 13.5 us -> 0.14 us
  other arithmetic: 12.1 us -> 0.63 us
  local copies, waits for them, and re-layouts: 3.08 us -> 9.14 us
    psum x2 -> x0, waiting for transfers between devices: 423 us -> none  [the longest x1 272 us: local(): factor = lax.psum(q_part, ('dp', 'tensor'))]
    all_to_all x0 -> x3, blocking collectives: none -> 36.7 us  [the longest x2 24.7 us: scatter_sum(): return jnp.sum(lax.all_to_all(chunks, axes, 0, 0), axis=0)]
    pallas_call x0 -> x6, Pallas kernels: none -> 25.5 us  [the longest x1 8.07 us: left_product(): pl.pallas_call(left_kernel, grid=(LEFT_STEPS,), in_specs=[pl.BlockSpec((s...]
    dot_general x5 -> x0, matrix products: 24.9 us -> none  [the longest x1 9.53 us: local(): lax.dot_general(merged, p_orth, first_dims, precision=highest_precision)]
    psum x1 -> x0, blocking collectives: 24.6 us -> none  [local(): gram_matrix = lax.psum(gram_part, 'tensor')]
    all_to_all x0 -> x3, starting transfers between devices: none -> 23 us  [spread(): return lax.all_to_all(copies, axes, 0, 0)]
    all_to_all x0 -> x3, waiting for transfers between devices: none -> 18.1 us  [spread(): return lax.all_to_all(copies, axes, 0, 0)]
    another operation x5 -> x0, other arithmetic: 12.1 us -> none  [the longest x3 6.52 us: local(): lower_factor = jnp.linalg.cholesky(gram_matrix)]
  transfers between devices with their start and end apart: 2 -> 4, of which waited for: 2 -> 3; matrix products, arithmetic and copies ran while one was open for 0% -> 0% of each run, Pallas kernels for 0% -> 10%
where the time goes in v2:
time: 124 us; the launch traced here: 123 us
  blocking collectives  40.6 us (33%)
  starting transfers between devices  28.8 us (23%)
  Pallas kernels  25.5 us (21%)
  waiting for transfers between devices  18.1 us (15%)
  local copies, waits for them, and re-layouts  9.14 us (7%)
    all_to_all x2, blocking collectives, scatter_sum(): return jnp.sum(lax.all_to_all(chunks, axes, 0, 0), axis=0)  24.7 us
    all_to_all x3, starting transfers between devices, spread(): return lax.all_to_all(copies, axes, 0, 0)  23 us
    all_to_all x3, waiting for transfers between devices, spread(): return lax.all_to_all(copies, axes, 0, 0)  18.1 us
    all_to_all x1, blocking collectives, spread(): return lax.all_to_all(copies, axes, 0, 0)  12 us
    pallas_call x1, Pallas kernels, left_product(): pl.pallas_call(left_kernel, grid=(LEFT_STEPS,), in_specs=[pl.BlockSpec((s...  8.07 us
    unnamed x10, local copies, waits for them, and re-layouts  6.84 us
    pallas_call x1, Pallas kernels, whiten(): pl.pallas_call(functools.partial(whiten_kernel, peers_of(NEAR)), out_shap...  6.04 us
    ppermute x1, starting transfers between devices, local(): both = kept + lax.ppermute(sent, 'core', [(0, 1), (1, 0)])  5.83 us
  transfers between devices with their start and end apart: 4, of which 3 were waited for; matrix products, arithmetic and copies ran while one was open for 0% of the time, Pallas kernels for 10%

profile of v2, /device:TPU:1, one launch (start us, length us, event | category | flops | bytes accessed | tf_op | source)
XLA Modules:
  0.0 122.9 jit_solution(9879324572438671069)
XLA Ops:
  0.0 8.1 %shard_map.46 = f32[64,384]{1,0:T(8,128)} custom-call(bf16[1024,384]{1,0:T(8,128)(2,1)} %act_ref.2, bf16[1024,2560]{1,0:T(8,128)(2,1)} %grad_ref.3, bf16[384,2560]{1,0:T(8,128)(2,1)} %bitcast.6, bf16[64,2560]{1,0:T(8,128)(2,1)} %bitcast.13), custom_call_target="tpu_custom_call" | custom-call | flops 335544320 | bytes 7208960 | tf_op jit(solution)/shard_map/pallas_call | solution.py:84
  8.1 9.1 %all_to_all.30 = f32[4,16,384]{2,1,0:T(8,128)S(1)} all-to-all(f32[4,16,384]{2,1,0:T(8,128)} %bitcast.12), channel_id=1, replica_groups=mesh['yA'=2,'yB'=2,'yC'=2,'zA'=2,'zB'=2,'zC'=2,'x'=4,'core'=2] {'yC','zC'}, dimensions={0} | all-to-all | bytes 196608 | tf_op jit(solution)/shard_map/all_to_all | solution.py:238
  17.2 0.8 broadcast_in_dim.8
  18.0 14.3 %all-to-all-start.1 = ((f32[16,16,384]{2,1,0:T(8,128)}), f32[16,16,384]{2,1,0:T(8,128)S(1)}, u32[]{:S(2)}, u32[]{:S(2)}) async-start(f32[16,16,384]{2,1,0:T(8,128)} %broadcast_in_dim.8), calls=%async_computation.1 | async-start | bytes 786432 | tf_op jit(solution)/shard_map/all_to_all | solution.py:243
  32.3 0.0 copy-done.4
  32.3 0.0 copy-start
  32.3 2.5 %copy-done = bf16[1024,2560]{1,0:T(8,128)(2,1)S(1)} copy-done((bf16[1024,2560]{1,0:T(8,128)(2,1)S(1)}, bf16[1024,2560]{1,0:T(8,128)(2,1)}, u32[]{:S(2)}) %copy-start) | copy-done | bytes 5242904
  34.8 1.5 %copy-done.3 = bf16[1,384,2560]{2,1,0:T(8,128)(2,1)S(1)} copy-done((bf16[1,384,2560]{2,1,0:T(8,128)(2,1)S(1)}, bf16[1,384,2560]{2,1,0:T(8,128)(2,1)}, u32[]{:S(2)}) %copy-start.3) | copy-done | bytes 1966104
  36.3 4.2 %shard_map.47 = (bf16[384,2560]{1,0:T(8,128)(2,1)S(1)}, bf16[384,2560]{1,0:T(8,128)(2,1)S(1)}) custom-call(bf16[1024,384]{1,0:T(8,128)(2,1)S(1)} %copy-done.4, bf16[1024,2560]{1,0:T(8,128)(2,1)S(1)} %copy-done, bf16[384,2560]{1,0:T(8,128)(2,1)S(1)} %bitcast.7), custom_call_target="tpu_custom_call" | custom-call | flops 2013265920 | bytes 11141120 | tf_op jit(solution)/shard_map/pallas_call | solution.py:117
  40.5 0.0 copy-start.1
  40.5 1.3 %copy-done.1 = bf16[384,2560]{1,0:T(8,128)(2,1)} copy-done((bf16[384,2560]{1,0:T(8,128)(2,1)}, bf16[384,2560]{1,0:T(8,128)(2,1)S(1)}, u32[]{:S(2)}) %copy-start.1) | copy-done | bytes 1966104
  41.8 5.7 %all-to-all-done.1 = f32[16,16,384]{2,1,0:T(8,128)S(1)} async-done(((f32[16,16,384]{2,1,0:T(8,128)}), f32[16,16,384]{2,1,0:T(8,128)S(1)}, u32[]{:S(2)}, u32[]{:S(2)}) %all-to-all-start.1) | async-done | bytes 393248 | tf_op jit(solution)/shard_map/all_to_all | solution.py:243
  47.5 0.6 broadcast_in_dim.9
  48.1 3.3 %all-to-all-start.2 = ((f32[4,16,384]{2,1,0:T(8,128)}), f32[4,16,384]{2,1,0:T(8,128)S(1)}, u32[]{:S(2)}, u32[]{:S(2)}) async-start(f32[4,16,384]{2,1,0:T(8,128)} %broadcast_in_dim.9), calls=%async_computation.2 | async-start | bytes 196608 | tf_op jit(solution)/shard_map/all_to_all | solution.py:243
  51.4 3.7 %all-to-all-done.2 = f32[4,16,384]{2,1,0:T(8,128)S(1)} async-done(((f32[4,16,384]{2,1,0:T(8,128)}), f32[4,16,384]{2,1,0:T(8,128)S(1)}, u32[]{:S(2)}, u32[]{:S(2)}) %all-to-all-start.2) | async-done | bytes 98336 | tf_op jit(solution)/shard_map/all_to_all | solution.py:243
  55.2 1.5 %copy-done.2 = bf16[384,2560]{1,0:T(8,128)(2,1)S(1)} copy-done((bf16[384,2560]{1,0:T(8,128)(2,1)S(1)}, bf16[384,2560]{1,0:T(8,128)(2,1)}, u32[]{:S(2)}) %copy-start.2) | copy-done | bytes 1966104
  56.7 2.0 %shard_map.49 = f32[16,2,4608]{2,1,0:T(2,128)S(1)} custom-call(s32[1]{0:T(128)S(6)} %sub.3.half_ref, f32[64,384]{1,0:T(8,128)S(1)} %bitcast.9, bf16[384,2560]{1,0:T(8,128)(2,1)S(1)} %get-tuple-element.19.high_ref, bf16[384,2560]{1,0:T(8,128)(2,1)S(1)} %copy-done.2), custom_call_target="tpu_custom_call" | custom-call | flops 188743680 | bytes 3932160 | tf_op jit(solution)/shard_map/pallas_call | solution.py:161
  58.7 5.8 %collective-permute-start = (f32[16,2,4608]{2,1,0:T(2,128)S(1)}, f32[16,2,4608]{2,1,0:T(2,128)S(1)}, u32[]{:S(2)}, u32[]{:S(2)}) collective-permute-start(f32[16,2,4608]{2,1,0:T(2,128)S(1)} %shard_map.49), channel_id=1, source_target_pairs={{0,1},{1,0},{2,3},{3,2},{4,5},{5,4},{6,7},{7,6},{8,9},{9,8},{10,11... | collective-permute-start | bytes 1769480 | tf_op jit(solution)/shard_map/ppermute | solution.py:263
  64.6 2.0 %shard_map.48 = f32[16,2,4608]{2,1,0:T(2,128)S(1)} custom-call(s32[1]{0:T(128)} %bitcast.half_ref, f32[64,384]{1,0:T(8,128)S(1)} %bitcast.10, bf16[384,2560]{1,0:T(8,128)(2,1)S(1)} %get-tuple-element.19.high_ref, bf16[384,2560]{1,0:T(8,128)(2,1)S(1)} %copy-done.2), custom_call_target="tpu_custom_call" | custom-call | flops 188743680 | bytes 3932160 | tf_op jit(solution)/shard_map/pallas_call | solution.py:161
  66.6 0.0 collective-permute-done
  66.6 0.3 add.3
  66.9 15.6 %all_to_all.31 = f32[16,2,4608]{2,1,0:T(2,128)S(1)} all-to-all(f32[16,2,4608]{2,1,0:T(2,128)S(1)} %add.3), channel_id=1, replica_groups=mesh['yA'=2,'yB'=2,'yC'=2,'zA'=2,'zB'=2,'zC'=2,'x'=4,'core'=2] {'yC','zC..., dimensions={0} | all-to-all | bytes 1179648 | tf_op jit(solution)/shard_map/all_to_all | solution.py:238
  82.5 0.2 reduce_sum.38.gram_ref
  82.7 0.8 broadcast_in_dim.10
  83.5 5.4 %all-to-all-start.4 = ((f32[16,2,2560]{2,1,0:T(2,128)}), f32[16,2,2560]{2,1,0:T(2,128)S(1)}, u32[]{:S(2)}, u32[]{:S(2)}) async-start(f32[16,2,2560]{2,1,0:T(2,128)} %broadcast_in_dim.10), calls=%async_computation.4 | async-start | bytes 655360 | tf_op jit(solution)/shard_map/all_to_all | solution.py:243
  88.9 6.0 %shard_map.50.scaled_ref = bf16[384,192]{1,0:T(8,128)(2,1)S(1)} custom-call(f32[2,4608]{1,0:T(2,128)S(1)} %reduce_sum.38.gram_ref, f32[64,384]{1,0:T(8,128)S(1)} %bitcast.11), custom_call_target="tpu_custom_call" | custom-call | flops 400000000 | bytes 4000000 | tf_op jit(solution)/shard_map/pallas_call | solution.py:202
  95.0 8.7 %all-to-all-done.4 = f32[16,2,2560]{2,1,0:T(2,128)S(1)} async-done(((f32[16,2,2560]{2,1,0:T(2,128)}), f32[16,2,2560]{2,1,0:T(2,128)S(1)}, u32[]{:S(2)}, u32[]{:S(2)}) %all-to-all-start.4) | async-done | bytes 327712 | tf_op jit(solution)/shard_map/all_to_all | solution.py:243
  103.7 0.1 reduce_sum.39
  103.8 0.1 broadcast_in_dim.11
  103.9 12.0 %all_to_all.32 = f32[16,2,2560]{2,1,0:T(2,128)S(1)} all-to-all(f32[16,2,2560]{2,1,0:T(2,128)S(1)} %broadcast_in_dim.11), channel_id=1, replica_groups=mesh['yA'=2,'yB'=2,'yC'=2,'zA'=2,'zB'=2,'zC'=2,'x'=4,'core'=2] {'yC','zC..., dimensions={0} | all-to-all | bytes 655360 | tf_op jit(solution)/shard_map/all_to_all | solution.py:243
  115.9 3.8 %all-gather = f32[32,2,2560]{2,1,0:T(2,128)S(1)} all-gather(f32[16,2,2560]{2,1,0:T(2,128)S(1)} %all_to_all.32), channel_id=2, replica_groups=mesh['yA'=2,'yB'=2,'yC'=2,'zA'=2,'zB'=2,'zC'=2,'x'=4,'core'=2] {'core'}, dimensions={0}, use_global_device_ids=true | all-gather | bytes 983040 | tf_op jit(solution)/shard_map/all_gather | solution.py:268
  119.7 3.2 %shard_map.51 = bf16[384,2560]{1,0:T(8,128)(2,1)} custom-call(bf16[384,192]{1,0:T(8,128)(2,1)S(1)} %shard_map.50.scaled_ref, f32[2,16,2,2560]{3,2,1,0:T(2,128)S(1)} %bitcast.8), custom_call_target="tpu_custom_call" | custom-call | flops 377487360 | bytes 1966080 | tf_op jit(solution)/shard_map/pallas_call | solution.py:219
  (6 shorter events, 0.0 us)
Async XLA Ops:
  8.1 24.2 %copy-start.4 = (bf16[1024,384]{1,0:T(8,128)(2,1)S(1)}, bf16[1024,384]{1,0:T(8,128)(2,1)}, u32[]{:S(2)}) copy-start(bf16[1024,384]{1,0:T(8,128)(2,1)} %act_ref.2) | copy-start | bytes 2359300
  18.0 29.5 %all-to-all-start.1 = ((f32[16,16,384]{2,1,0:T(8,128)}), f32[16,16,384]{2,1,0:T(8,128)S(1)}, u32[]{:S(2)}, u32[]{:S(2)}) async-start(f32[16,16,384]{2,1,0:T(8,128)} %broadcast_in_dim.8), calls=%async_computation.1 | async-start | bytes 786432 | tf_op jit(solution)/shard_map/all_to_all | solution.py:243
  32.3 2.5 %copy-start = (bf16[1024,2560]{1,0:T(8,128)(2,1)S(1)}, bf16[1024,2560]{1,0:T(8,128)(2,1)}, u32[]{:S(2)}) copy-start(bf16[1024,2560]{1,0:T(8,128)(2,1)} %grad_ref.3) | copy-start | bytes 15728644
  34.8 1.5 %copy-start.3 = (bf16[1,384,2560]{2,1,0:T(8,128)(2,1)S(1)}, bf16[1,384,2560]{2,1,0:T(8,128)(2,1)}, u32[]{:S(2)}) copy-start(bf16[1,384,2560]{2,1,0:T(8,128)(2,1)} %param.6) | copy-start | bytes 5898244
  40.5 1.3 %copy-start.1 = (bf16[384,2560]{1,0:T(8,128)(2,1)}, bf16[384,2560]{1,0:T(8,128)(2,1)S(1)}, u32[]{:S(2)}) copy-start(bf16[384,2560]{1,0:T(8,128)(2,1)S(1)} %get-tuple-element.20.low_ref) | copy-start | bytes 5898244
  48.1 7.1 %all-to-all-start.2 = ((f32[4,16,384]{2,1,0:T(8,128)}), f32[4,16,384]{2,1,0:T(8,128)S(1)}, u32[]{:S(2)}, u32[]{:S(2)}) async-start(f32[4,16,384]{2,1,0:T(8,128)} %broadcast_in_dim.9), calls=%async_computation.2 | async-start | bytes 196608 | tf_op jit(solution)/shard_map/all_to_all | solution.py:243
  55.2 1.5 %copy-start.2 = (bf16[384,2560]{1,0:T(8,128)(2,1)S(1)}, bf16[384,2560]{1,0:T(8,128)(2,1)}, u32[]{:S(2)}) copy-start(bf16[384,2560]{1,0:T(8,128)(2,1)} %copy-done.1) | copy-start | bytes 5898244
  58.7 7.9 %collective-permute-start = (f32[16,2,4608]{2,1,0:T(2,128)S(1)}, f32[16,2,4608]{2,1,0:T(2,128)S(1)}, u32[]{:S(2)}, u32[]{:S(2)}) collective-permute-start(f32[16,2,4608]{2,1,0:T(2,128)S(1)} %shard_map.49), channel_id=1, source_target_pairs={{0,1},{1,0},{2,3},{3,2},{4,5},{5,4},{6,7},{7,6},{8,9},{9,8},{10,11... | collective-permute-start | bytes 1769480 | tf_op jit(solution)/shard_map/ppermute | solution.py:263
  83.5 20.1 %all-to-all-start.4 = ((f32[16,2,2560]{2,1,0:T(2,128)}), f32[16,2,2560]{2,1,0:T(2,128)S(1)}, u32[]{:S(2)}, u32[]{:S(2)}) async-start(f32[16,2,2560]{2,1,0:T(2,128)} %broadcast_in_dim.10), calls=%async_computation.4 | async-start | bytes 655360 | tf_op jit(solution)/shard_map/all_to_all | solution.py:243

commit v3 on v0

v3 whole, which is shorter than its diff:
```python
import math

import jax
import jax.numpy as jnp
from jax import lax
from jax.experimental import pallas as pl
from jax.experimental.pallas import tpu as pltpu
from jax.sharding import Mesh, PartitionSpec as P

RANK = 64
HALF = RANK // 2
LANES = 2 * RANK
PARTS = 2
GRID = {"yA": 2, "yB": 2, "yC": 2, "zA": 2, "zB": 2, "zC": 2, "x": 4, "core": 2}
DP = ("yA", "yB", "yC", "zA", "zB", "zC")
TENSOR = ("x", "core")
Y, Z = DP[:3], DP[3:]
NEAR = ("yC", "zC")
NEAR_X = ("yC", "zC", "x")
FAR = ("yA", "yB", "zA", "zB")

highest_precision = lax.Precision.HIGHEST
plain_dims = (((1,), (0,)), ((), ()))
first_dims = (((0,), (0,)), ((), ()))
last_dims = (((1,), (1,)), ((), ()))


def dot32(left, right, dims=plain_dims):
    return lax.dot_general(left, right, dims, preferred_element_type=jnp.float32)


def dot_exact(left, right, dims=plain_dims):
    return lax.dot_general(
        left, right, dims, precision=highest_precision, preferred_element_type=jnp.float32
    )


def split(value, terms):
    parts = []
    for _ in range(terms):
        part = lax.reduce_precision(value, 8, 7)
        parts.append(part.astype(jnp.bfloat16))
        value = value - part
    return parts


def kernel_split(value, terms):
    parts = []
    for _ in range(terms):
        part = value.astype(jnp.bfloat16)
        parts.append(part)
        value = value - part.astype(jnp.float32)
    return parts


def peers_of(axes):
    return math.prod(GRID[axis] for axis in axes)


def params(megabytes):
    return pltpu.CompilerParams(vmem_limit_bytes=megabytes * 1024 * 1024)


def cost(flops, moved):
    return pl.CostEstimate(flops=flops, bytes_accessed=moved, transcendentals=0)


WHOLE = pl.BlockSpec(memory_space=pltpu.VMEM)


def left_product(activations, out_grads, residue, warm_start):
    projected = jnp.concatenate(split(dot32(out_grads, warm_start), 3), axis=1)
    terms = dot32(projected, activations, first_dims)
    left = terms[:RANK] + terms[RANK : 2 * RANK] + terms[2 * RANK :]
    return left + dot32(warm_start, residue, (((0,), (1,)), ((), ())))


def merged_kernel(act_ref, grad_ref, res_ref, out_ref, act_t):
    @pl.when(pl.program_id(0) == 0)
    def _():
        act_t[...] = act_ref[...].T

    merged = dot32(act_t[...], grad_ref[...]) + res_ref[...].astype(jnp.float32)
    out_ref[0], out_ref[1] = kernel_split(merged, 2)


def merged_terms(activations, out_grads, residue, part):
    tokens, rows = activations.shape
    cols = out_grads.shape[1] // PARTS
    steps = 2
    block, first = cols // steps, part * steps
    return pl.pallas_call(
        merged_kernel,
        grid=(steps,),
        in_specs=[
            pl.BlockSpec((tokens, rows), lambda i: (0, 0)),
            pl.BlockSpec((tokens, block), lambda i: (0, first + i)),
            pl.BlockSpec((rows, block), lambda i: (0, first + i)),
        ],
        out_specs=pl.BlockSpec((2, rows, block), lambda i: (0, 0, i)),
        out_shape=jax.ShapeDtypeStruct((2, rows, cols), jnp.bfloat16),
        scratch_shapes=[pltpu.VMEM((rows, tokens), jnp.bfloat16)],
        compiler_params=params(60),
        cost_estimate=cost(2 * tokens * cols * rows, 2 * cols * (tokens + 3 * rows)),
    )(activations, out_grads, residue)


def right_kernel(left_ref, *refs):
    *terms_refs, kept_ref, sent_ref = refs
    cols = sum(terms_ref.shape[2] for terms_ref in terms_refs)
    peers, pair, _ = kept_ref.shape
    left = left_ref[...]
    swapped = jnp.concatenate([left[HALF:], left[:HALF]], axis=0)
    high, low = kernel_split(jnp.where(lax.axis_index("core") == 0, left, swapped), 2)
    stacked = jnp.concatenate([high, low], axis=0)
    block = terms_refs[0].shape[2] // 2
    for i in range(cols // block):
        terms_ref, place = terms_refs[i // 2], slice(i % 2 * block, (i % 2 + 1) * block)
        both = dot32(stacked, terms_ref[0, :, place])
        product = both[:RANK] + (both[RANK:] + dot32(high, terms_ref[1, :, place]))
        place = slice(i * block, (i + 1) * block)
        kept_ref[:, :, place] = product[:HALF].reshape(peers, pair, block)
        sent_ref[:, :, place] = product[HALF:].reshape(peers, pair, block)

    gram = dot_exact(left, left, last_dims)
    gram = jnp.concatenate([gram[:HALF], gram[HALF:]], axis=1)
    shares = peers_of(NEAR)
    height = HALF // shares
    share = gram[:height]
    mine = lax.axis_index(NEAR)
    for other in range(1, shares):
        share = jnp.where(mine == other, gram[other * height : (other + 1) * height], share)
    for i in range(height // pair):
        place = slice(cols + i * LANES, cols + (i + 1) * LANES)
        piece = jnp.broadcast_to(share[i * pair : (i + 1) * pair][None], (peers, pair, LANES))
        kept_ref[:, :, place] = piece
        sent_ref[:, :, place] = piece


def right_product(left, terms):
    rows, cols = left.shape[1], sum(part.shape[2] for part in terms)
    peers = peers_of(NEAR_X)
    shape = (peers, HALF // peers, cols + LANES * GRID["x"])
    return pl.pallas_call(
        right_kernel,
        in_specs=[WHOLE] * (1 + len(terms)),
        out_specs=[WHOLE] * 2,
        out_shape=[jax.ShapeDtypeStruct(shape, jnp.float32)] * 2,
        compiler_params=params(16),
        cost_estimate=cost(6 * rows * cols * RANK, 4 * cols * rows),
    )(left, *terms)


def whiten_kernel(gram_ref, left_ref, out_ref):
    shares, sources, pair = peers_of(NEAR), GRID["x"], gram_ref.shape[1]
    pieces = []
    for share in range(shares):
        for i in range(HALF // shares // pair):
            place = slice(i * LANES, (i + 1) * LANES)
            first = share * sources
            piece = gram_ref[first, :, place]
            for source in range(1, sources):
                piece = piece + gram_ref[first + source, :, place]
            pieces.append(piece)
    gram = jnp.concatenate(pieces, axis=0)
    gram = jnp.concatenate([gram[:, :RANK], gram[:, RANK:]], axis=0)
    row = lax.broadcasted_iota(jnp.int32, (RANK, RANK), 0)
    col = lax.broadcasted_iota(jnp.int32, (RANK, RANK), 1)
    work = jnp.concatenate([gram, (row == col).astype(jnp.float32)], axis=1)
    tall = lax.broadcasted_iota(jnp.int32, (RANK, 2 * RANK), 0)
    for k in range(RANK - 1):
        pivot = work[k : k + 1, :]
        scale = work[:, k : k + 1] / pivot[:, k : k + 1]
        work = jnp.where(tall > k, work - scale * pivot, work)
    inverse = work[:, RANK:]
    diagonal = jnp.sum(jnp.where(row == col, work[:, :RANK], 0.0), axis=1, keepdims=True)
    basis = dot_exact(inverse, left_ref[...])
    scaled = dot_exact(basis, inverse / diagonal, first_dims)
    high, low = kernel_split(scaled, 2)
    out_ref[...] = jnp.concatenate([high, high, low], axis=1)


def whiten(chunks, left):
    rows = left.shape[1]
    width = LANES * GRID["x"]
    last = chunks.shape[2] // width - 1
    return pl.pallas_call(
        whiten_kernel,
        grid=(1,),
        in_specs=[
            pl.BlockSpec((*chunks.shape[:2], width), lambda i: (0, 0, last)),
            pl.BlockSpec(left.shape, lambda i: (0, 0)),
        ],
        out_specs=pl.BlockSpec((rows, 3 * RANK), lambda i: (0, 0)),
        out_shape=jax.ShapeDtypeStruct((rows, 3 * RANK), jnp.bfloat16),
        compiler_params=params(16),
        cost_estimate=cost(400_000_000, 4_000_000),
    )(chunks, left)


def update_kernel(scaled_ref, right_ref, out_ref, held, sems):
    block = 512
    copies = []
    for i in range(held.shape[1] // block):
        place = slice(i * block, (i + 1) * block)
        high, low = kernel_split(right_ref[:, :, :, place].reshape(RANK, block), 2)
        terms = jnp.concatenate([high, low, high], axis=0)
        held[:, place] = dot32(scaled_ref[...], terms).astype(jnp.bfloat16)
        place = pl.ds(i * block, block)
        copies.append(pltpu.make_async_copy(held.at[:, place], out_ref.at[:, place], sems.at[i]))
        copies[-1].start()
    for copy in copies:
        copy.wait()


def update_product(scaled, right):
    rows, cols = scaled.shape[0], right.shape[-1]
    return pl.pallas_call(
        update_kernel,
        in_specs=[WHOLE] * 2,
        out_specs=pl.BlockSpec(memory_space=pl.ANY),
        out_shape=jax.ShapeDtypeStruct((rows, cols), jnp.bfloat16),
        scratch_shapes=[
            pltpu.VMEM((rows, cols), jnp.bfloat16),
            pltpu.SemaphoreType.DMA((cols // 512,)),
        ],
        compiler_params=params(16),
        cost_estimate=cost(6 * rows * cols * RANK, 2 * cols * rows),
    )(scaled, right)


def copies_kernel(chunks_ref, out_ref):
    total = chunks_ref[0]
    for peer in range(1, chunks_ref.shape[0]):
        total = total + chunks_ref[peer]
    for peer in range(out_ref.shape[0]):
        out_ref[peer] = total


def sum_copies(chunks, axes, cols):
    sources, rows, _ = chunks.shape
    shape = (peers_of(axes), rows, cols)
    return pl.pallas_call(
        copies_kernel,
        grid=(1,),
        in_specs=[pl.BlockSpec((sources, rows, cols), lambda i: (0, 0, 0))],
        out_specs=pl.BlockSpec(shape, lambda i: (0, 0, 0)),
        out_shape=pltpu.VMEM(shape, jnp.float32),
        compiler_params=params(8),
        cost_estimate=cost(sources * rows * cols, 4 * sources * rows * cols),
    )(chunks)


def exchange(chunks, axes):
    return lax.all_to_all(chunks, axes, 0, 0)


def after(first, *values):
    return lax.optimization_barrier((first, *values))


def local(activations, out_grads, residue, warm_start):
    residue = residue[0]
    rows, cols = residue.shape
    core = lax.axis_index("core")
    left = left_product(activations, out_grads, residue, warm_start)
    left, activations, is_first = after(left, activations, core == 0)
    terms_a = merged_terms(activations, out_grads, residue, 0)
    left = exchange(left.reshape(peers_of(Z), -1, rows), Z)
    left, terms_a, activations = after(sum_copies(left, Y, rows), terms_a, activations)
    terms_b = merged_terms(activations, out_grads, residue, 1)
    left, terms_b = after(sum_copies(exchange(left, Y), Z, rows), terms_b)
    left = exchange(left, Z).reshape(RANK, rows)

    kept, sent = right_product(left, [terms_a, terms_b])
    sent = lax.all_gather(sent, "core", axis=0)
    chunks = exchange(kept + jnp.where(is_first, sent[1], sent[0]), NEAR_X)
    scaled = whiten(chunks, left)
    right = exchange(sum_copies(chunks, FAR, cols), FAR)
    right, scaled = after(sum_copies(right, NEAR_X, cols), scaled)
    right = lax.all_gather(exchange(right, NEAR_X), "core", axis=0)
    return update_product(scaled, right)


def solution(mesh):
    fine = Mesh(mesh.devices.reshape(*GRID.values()), tuple(GRID))
    in_specs = (P(DP, TENSOR), P(DP, None), P(DP, TENSOR, None), P())
    return jax.shard_map(local, mesh=fine, in_specs=in_specs, out_specs=P(TENSOR, None), check_vma=False)
```

time: 504 us -> 110 us (0.22)
  waiting for transfers between devices: 424 us -> 14 us
  starting transfers between devices: 0.04 us -> 21.5 us
  blocking collectives: 24.6 us -> 45.8 us
  matrix products: 26.1 us -> 6.09 us
  Pallas kernels: 0 us -> 19.6 us
  between operations: 13.5 us -> 0.08 us
  other arithmetic: 12.1 us -> 0.27 us
    psum x2 -> x0, waiting for transfers between devices: 423 us -> none  [the longest x1 272 us: local(): factor = lax.psum(q_part, ('dp', 'tensor'))]
    all_to_all x0 -> x3, blocking collectives: none -> 34.2 us  [exchange(): return lax.all_to_all(chunks, axes, 0, 0)]
    psum x1 -> x0, blocking collectives: 24.6 us -> none  [local(): gram_matrix = lax.psum(gram_part, 'tensor')]
    all_to_all x0 -> x3, starting transfers between devices: none -> 21.5 us  [exchange(): return lax.all_to_all(chunks, axes, 0, 0)]
    pallas_call x0 -> x9, Pallas kernels: none -> 19.6 us  [the longest x2 9.32 us: merged_terms(): pl.pallas_call(merged_kernel, grid=(steps,), in_specs=[pl.BlockSpec((toke...]
    dot_general x5 -> x3, matrix products: 24.9 us -> 6.09 us  [dot32(): lax.dot_general(left, right, dims, preferred_element_type=jnp.float32)]
    all_to_all x0 -> x3, waiting for transfers between devices: none -> 14 us  [exchange(): return lax.all_to_all(chunks, axes, 0, 0)]
    another operation x5 -> x0, other arithmetic: 12.1 us -> none  [the longest x3 6.52 us: local(): lower_factor = jnp.linalg.cholesky(gram_matrix)]
  transfers between devices with their start and end apart: 2 -> 3, of which waited for: 2 -> 3; matrix products, arithmetic and copies ran while one was open for 0% -> 0% of each run, Pallas kernels for 0% -> 14%
where the time goes in v3:
time: 110 us
  blocking collectives  45.8 us (42%)
  starting transfers between devices  21.5 us (20%)
  Pallas kernels  19.6 us (18%)
  waiting for transfers between devices  14 us (13%)
  matrix products  6.09 us (6%)
  local copies, waits for them, and re-layouts  2.53 us (2%)
    all_to_all x3, blocking collectives, exchange(): return lax.all_to_all(chunks, axes, 0, 0)  34.2 us
    all_to_all x3, starting transfers between devices, exchange(): return lax.all_to_all(chunks, axes, 0, 0)  21.5 us
    all_to_all x3, waiting for transfers between devices, exchange(): return lax.all_to_all(chunks, axes, 0, 0)  14 us
    pallas_call x2, Pallas kernels, merged_terms(): pl.pallas_call(merged_kernel, grid=(steps,), in_specs=[pl.BlockSpec((toke...  9.32 us
    dot_general x3, matrix products, dot32(): lax.dot_general(left, right, dims, preferred_element_type=jnp.float32)  6.09 us
    pallas_call x1, Pallas kernels, whiten(): pl.pallas_call(whiten_kernel, grid=(1,), in_specs=[pl.BlockSpec((*chunks....  6.04 us
    all_gather x1, blocking collectives, local(): sent = lax.all_gather(sent, 'core', axis=0)  5.99 us
    all_gather x1, blocking collectives, local(): right = lax.all_gather(exchange(right, NEAR_X), 'core', axis=0)  5.62 us
  transfers between devices with their start and end apart: 3, of which 3 were waited for; matrix products, arithmetic and copies ran while one was open for 0% of the time, Pallas kernels for 14%

profile of v3, /device:TPU:1, one launch (start us, length us, event | category | flops | bytes accessed | tf_op | source)
XLA Modules:
  0.0 109.9 jit_solution(11100946405697309595)
XLA Ops:
  0.0 0.0 copy-start
  0.0 1.0 copy-done
  1.0 0.0 copy-start.4
  1.0 0.0 copy-start.3
  1.0 4.3 %reduce-precision_convert_fusion.1 = (bf16[1024,64]{0,1:T(8,128)(2,1)S(1)}, bf16[1024,64]{0,1:T(8,128)(2,1)S(1)}, bf16[1024,64]{0,1:T(8,128)(2,1)S(1)}) fusion(bf16[1024,2560]{1,0:T(8,128)(2,1)} %grad_ref.3, bf16[2560,64]{0,1:T(8,128)(2,1)S(1)} %copy-done), kind=kOutput, calls=%fused_computation.12 | convolution fusion | flops 336068608 | bytes 5963776 | tf_op jit(solution)/shard_map/dot_general | solution.py:29
  5.3 0.0 copy-done.4
  5.3 0.4 fusion.1
  5.7 0.0 copy-done.3
  5.7 1.4 %convolution_add_fusion = f32[64,384]{1,0:T(8,128)} fusion(bf16[2560,64]{0,1:T(8,128)(2,1)S(1)} %copy-done, f32[192,384]{1,0:T(8,128)S(1)} %fusion.1, bf16[1,384,2560]{2,1,0:T(8,128)(2,1)S(1)} %copy-done.3), kind=kOutput, calls=%fused_computation | convolution fusion | flops 125902848 | bytes 2686976 | tf_op jit(solution)/shard_map/dot_general | solution.py:29
  7.1 10.9 %all-to-all-start = ((f32[8,8,384]{2,1,0:T(8,128)}), f32[8,8,384]{2,1,0:T(8,128)S(1)}, u32[]{:S(2)}, u32[]{:S(2)}) async-start(f32[8,8,384]{2,1,0:T(8,128)} %bitcast.1), calls=%async_computation | async-start | bytes 196608 | tf_op jit(solution)/shard_map/all_to_all | solution.py:255
  18.0 4.5 %shard_map.47.refs_0_ = bf16[2,384,1280]{2,1,0:T(8,128)(2,1)} custom-call(bf16[1024,384]{1,0:T(8,128)(2,1)} %act_ref.1, bf16[1024,2560]{1,0:T(8,128)(2,1)} %grad_ref.3, bf16[384,2560]{1,0:T(8,128)(2,1)} %bitcast.13), custom_call_target="tpu_custom_call" | custom-call | flops 1006632960 | bytes 5570560 | tf_op jit(solution)/shard_map/pallas_call | solution.py:92
  22.5 3.1 %all-to-all-done.chunks_ref = f32[8,8,384]{2,1,0:T(8,128)S(1)} async-done(((f32[8,8,384]{2,1,0:T(8,128)}), f32[8,8,384]{2,1,0:T(8,128)S(1)}, u32[]{:S(2)}, u32[]{:S(2)}) %all-to-all-start) | async-done | bytes 98336 | tf_op jit(solution)/shard_map/all_to_all | solution.py:255
  25.6 0.6 shard_map.46
  26.2 6.8 %all-to-all-start.1 = ((f32[8,8,384]{2,1,0:T(8,128)}), f32[8,8,384]{2,1,0:T(8,128)S(1)}, u32[]{:S(2)}, u32[]{:S(2)}) async-start(f32[8,8,384]{2,1,0:T(8,128)} %shard_map.46), calls=%async_computation.1 | async-start | bytes 196608 | tf_op jit(solution)/shard_map/all_to_all | solution.py:255
  33.1 0.0 copy-start.1
  33.1 4.8 %shard_map.49.refs_1_ = bf16[2,384,1280]{2,1,0:T(8,128)(2,1)} custom-call(bf16[1024,384]{1,0:T(8,128)(2,1)} %act_ref.1, bf16[1024,2560]{1,0:T(8,128)(2,1)} %grad_ref.3, bf16[384,2560]{1,0:T(8,128)(2,1)} %bitcast.14), custom_call_target="tpu_custom_call" | custom-call | flops 1006632960 | bytes 5570560 | tf_op jit(solution)/shard_map/pallas_call | solution.py:92
  37.8 2.8 %all-to-all-done.1.chunks_ref = f32[8,8,384]{2,1,0:T(8,128)S(1)} async-done(((f32[8,8,384]{2,1,0:T(8,128)}), f32[8,8,384]{2,1,0:T(8,128)S(1)}, u32[]{:S(2)}, u32[]{:S(2)}) %all-to-all-start.1) | async-done | bytes 98336 | tf_op jit(solution)/shard_map/all_to_all | solution.py:255
  40.7 11.0 %all_to_all.30 = f32[8,8,384]{2,1,0:T(8,128)S(1)} all-to-all(f32[8,8,384]{2,1,0:T(8,128)S(1)} %shard_map.48), channel_id=1, replica_groups=mesh['yA'=2,'yB'=2,'yC'=2,'zA'=2,'zB'=2,'zC'=2,'x'=4,'core'=2] {'zA','zB..., dimensions={0} | all-to-all | bytes 196608 | tf_op jit(solution)/shard_map/all_to_all | solution.py:255
  51.7 0.0 copy-done.1
  51.7 0.0 copy-start.2
  51.7 1.5 %copy-done.2 = bf16[2,384,1280]{2,1,0:T(8,128)(2,1)S(1)} copy-done((bf16[2,384,1280]{2,1,0:T(8,128)(2,1)S(1)}, bf16[2,384,1280]{2,1,0:T(8,128)(2,1)}, u32[]{:S(2)}) %copy-start.2) | copy-done | bytes 1966104
  53.2 1.1 %shard_map.50 = (f32[16,2,3072]{2,1,0:T(2,128)S(1)}, f32[16,2,3072]{2,1,0:T(2,128)S(1)}) custom-call(f32[64,384]{1,0:T(8,128)S(1)} %bitcast.11, bf16[2,384,1280]{2,1,0:T(8,128)(2,1)S(1)} %copy-done.1, bf16[2,384,1280]{2,1,0:T(8,128)(2,1)S(1)} %copy-done.2), custom_call_target="tpu_custom_call" | custom-call | flops 377487360 | bytes 3932160 | tf_op jit(solution)/shard_map/pallas_call | solution.py:144
  54.4 6.0 %all-gather = f32[32,2,3072]{2,1,0:T(2,128)S(1)} all-gather(f32[16,2,3072]{2,1,0:T(2,128)S(1)} %get-tuple-element.26), channel_id=2, replica_groups=mesh['yA'=2,'yB'=2,'yC'=2,'zA'=2,'zB'=2,'zC'=2,'x'=4,'core'=2] {'core'}, dimensions={0}, use_global_device_ids=true | all-gather | bytes 1179648 | tf_op jit(solution)/shard_map/all_gather | solution.py:276
  60.4 0.3 fusion
  60.7 12.8 %all_to_all.31.chunks_ref.gram_ref = f32[16,2,3072]{2,1,0:T(2,128)S(1)} all-to-all(f32[16,2,3072]{2,1,0:T(2,128)S(1)} %fusion), channel_id=1, replica_groups=mesh['yA'=2,'yB'=2,'yC'=2,'zA'=2,'zB'=2,'zC'=2,'x'=4,'core'=2] {'yC','zC..., dimensions={0} | all-to-all | bytes 786432 | tf_op jit(solution)/shard_map/all_to_all | solution.py:255
  73.5 0.8 shard_map.51
  74.3 3.8 %all-to-all-start.4 = ((f32[16,2,2560]{2,1,0:T(2,128)}), f32[16,2,2560]{2,1,0:T(2,128)S(1)}, u32[]{:S(2)}, u32[]{:S(2)}) async-start(f32[16,2,2560]{2,1,0:T(2,128)} %shard_map.51), calls=%async_computation.4 | async-start | bytes 655360 | tf_op jit(solution)/shard_map/all_to_all | solution.py:255
  78.1 6.0 %shard_map.53.scaled_ref = bf16[384,192]{1,0:T(8,128)(2,1)S(1)} custom-call(f32[16,2,3072]{2,1,0:T(2,128)S(1)} %all_to_all.31.chunks_ref.gram_ref, f32[64,384]{1,0:T(8,128)S(1)} %bitcast.12), custom_call_target="tpu_custom_call" | custom-call | flops 400000000 | bytes 4000000 | tf_op jit(solution)/shard_map/pallas_call | solution.py:187
  84.1 8.2 %all-to-all-done.4.chunks_ref = f32[16,2,2560]{2,1,0:T(2,128)S(1)} async-done(((f32[16,2,2560]{2,1,0:T(2,128)}), f32[16,2,2560]{2,1,0:T(2,128)S(1)}, u32[]{:S(2)}, u32[]{:S(2)}) %all-to-all-start.4) | async-done | bytes 327712 | tf_op jit(solution)/shard_map/all_to_all | solution.py:255
  92.4 10.3 %all_to_all.32 = f32[16,2,2560]{2,1,0:T(2,128)S(1)} all-to-all(f32[16,2,2560]{2,1,0:T(2,128)S(1)} %shard_map.52), channel_id=1, replica_groups=mesh['yA'=2,'yB'=2,'yC'=2,'zA'=2,'zB'=2,'zC'=2,'x'=4,'core'=2] {'yC','zC..., dimensions={0} | all-to-all | bytes 655360 | tf_op jit(solution)/shard_map/all_to_all | solution.py:255
  102.7 5.6 %all-gather.1 = f32[32,2,2560]{2,1,0:T(2,128)S(1)} all-gather(f32[16,2,2560]{2,1,0:T(2,128)S(1)} %all_to_all.32), channel_id=3, replica_groups=mesh['yA'=2,'yB'=2,'yC'=2,'zA'=2,'zB'=2,'zC'=2,'x'=4,'core'=2] {'core'}, dimensions={0}, use_global_device_ids=true | all-gather | bytes 983040 | tf_op jit(solution)/shard_map/all_gather | solution.py:281
  108.3 1.6 %shard_map.54 = bf16[384,2560]{1,0:T(8,128)(2,1)} custom-call(bf16[384,192]{1,0:T(8,128)(2,1)S(1)} %shard_map.53.scaled_ref, f32[2,16,2,2560]{3,2,1,0:T(2,128)S(1)} %bitcast.10), custom_call_target="tpu_custom_call" | custom-call | flops 377487360 | bytes 1966080 | tf_op jit(solution)/shard_map/pallas_call | solution.py:218
  (2 shorter events, 0.1 us)
Async XLA Ops:
  0.0 1.0 copy-start
  1.0 4.3 %copy-start.4 = (bf16[1024,384]{1,0:T(8,128)(2,1)S(1)}, bf16[1024,384]{1,0:T(8,128)(2,1)}, u32[]{:S(2)}) copy-start(bf16[1024,384]{1,0:T(8,128)(2,1)} %act_ref.1) | copy-start | bytes 2359300
  1.0 4.7 %copy-start.3 = (bf16[1,384,2560]{2,1,0:T(8,128)(2,1)S(1)}, bf16[1,384,2560]{2,1,0:T(8,128)(2,1)}, u32[]{:S(2)}) copy-start(bf16[1,384,2560]{2,1,0:T(8,128)(2,1)} %param.6) | copy-start | bytes 5898244
  7.1 18.5 %all-to-all-start = ((f32[8,8,384]{2,1,0:T(8,128)}), f32[8,8,384]{2,1,0:T(8,128)S(1)}, u32[]{:S(2)}, u32[]{:S(2)}) async-start(f32[8,8,384]{2,1,0:T(8,128)} %bitcast.1), calls=%async_computation | async-start | bytes 196608 | tf_op jit(solution)/shard_map/all_to_all | solution.py:255
  26.2 14.4 %all-to-all-start.1 = ((f32[8,8,384]{2,1,0:T(8,128)}), f32[8,8,384]{2,1,0:T(8,128)S(1)}, u32[]{:S(2)}, u32[]{:S(2)}) async-start(f32[8,8,384]{2,1,0:T(8,128)} %shard_map.46), calls=%async_computation.1 | async-start | bytes 196608 | tf_op jit(solution)/shard_map/all_to_all | solution.py:255
  33.1 18.6 %copy-start.1 = (bf16[2,384,1280]{2,1,0:T(8,128)(2,1)S(1)}, bf16[2,384,1280]{2,1,0:T(8,128)(2,1)}, u32[]{:S(2)}) copy-start(bf16[2,384,1280]{2,1,0:T(8,128)(2,1)} %shard_map.47.refs_0_) | copy-start | bytes 5898244
  51.7 1.5 %copy-start.2 = (bf16[2,384,1280]{2,1,0:T(8,128)(2,1)S(1)}, bf16[2,384,1280]{2,1,0:T(8,128)(2,1)}, u32[]{:S(2)}) copy-start(bf16[2,384,1280]{2,1,0:T(8,128)(2,1)} %shard_map.49.refs_1_) | copy-start | bytes 5898244
  74.3 18.1 %all-to-all-start.4 = ((f32[16,2,2560]{2,1,0:T(2,128)}), f32[16,2,2560]{2,1,0:T(2,128)S(1)}, u32[]{:S(2)}, u32[]{:S(2)}) async-start(f32[16,2,2560]{2,1,0:T(2,128)} %shard_map.51), calls=%async_computation.4 | async-start | bytes 655360 | tf_op jit(solution)/shard_map/all_to_all | solution.py:255

commit v4 on v3

--- a/solution.py
+++ b/solution.py
@@ -10,7 +10,7 @@
 RANK = 64
 HALF = RANK // 2
 LANES = 2 * RANK
-PARTS = 2
+GRAD_BLOCKS = 2
 GRID = {"yA": 2, "yB": 2, "yC": 2, "zA": 2, "zB": 2, "zC": 2, "x": 4, "core": 2}
 DP = ("yA", "yB", "yC", "zA", "zB", "zC")
 TENSOR = ("x", "core")
@@ -68,57 +68,63 @@
 WHOLE = pl.BlockSpec(memory_space=pltpu.VMEM)
 
 
+def left_kernel(act_hbm, grad_hbm, res_hbm, warm_hbm, out_ref, act_ref, grad_ref, res_ref, warm_ref, sems):
+    tokens = grad_ref.shape[0]
+    block = tokens // GRAD_BLOCKS
+    places = [pl.ds(i * block, block) for i in range(GRAD_BLOCKS)]
+    moves = [(warm_hbm, warm_ref), (res_hbm, res_ref)]
+    moves += [(grad_hbm.at[place], grad_ref.at[place]) for place in places]
+    moves += [(act_hbm, act_ref)]
+    copies = [pltpu.make_async_copy(*move, sems.at[i]) for i, move in enumerate(moves)]
+    for copy in copies:
+        copy.start()
+    copies[0].wait()
+    warm = warm_ref[...]
+    copies[1].wait()
+    left = dot32(warm, res_ref[...], last_dims)
+    projected = []
+    for i, place in enumerate(places):
+        copies[2 + i].wait()
+        terms = kernel_split(dot32(warm, grad_ref[place, :], last_dims), 3)
+        projected.append(jnp.concatenate(terms, axis=0))
+    copies[-1].wait()
+    terms = dot32(jnp.concatenate(projected, axis=1), act_ref[...])
+    out_ref[...] = terms[:RANK] + (terms[RANK : 2 * RANK] + terms[2 * RANK :]) + left
+
+
 def left_product(activations, out_grads, residue, warm_start):
-    projected = jnp.concatenate(split(dot32(out_grads, warm_start), 3), axis=1)
-    terms = dot32(projected, activations, first_dims)
-    left = terms[:RANK] + terms[RANK : 2 * RANK] + terms[2 * RANK :]
-    return left + dot32(warm_start, residue, (((0,), (1,)), ((), ())))
-
-
-def merged_kernel(act_ref, grad_ref, res_ref, out_ref, act_t):
-    @pl.when(pl.program_id(0) == 0)
-    def _():
-        act_t[...] = act_ref[...].T
-
-    merged = dot32(act_t[...], grad_ref[...]) + res_ref[...].astype(jnp.float32)
-    out_ref[0], out_ref[1] = kernel_split(merged, 2)
-
-
-def merged_terms(activations, out_grads, residue, part):
     tokens, rows = activations.shape
-    cols = out_grads.shape[1] // PARTS
-    steps = 2
-    block, first = cols // steps, part * steps
-    return pl.pallas_call(
-        merged_kernel,
-        grid=(steps,),
-        in_specs=[
-            pl.BlockSpec((tokens, rows), lambda i: (0, 0)),
-            pl.BlockSpec((tokens, block), lambda i: (0, first + i)),
-            pl.BlockSpec((rows, block), lambda i: (0, first + i)),
+    cols = out_grads.shape[1]
+    arrays = [activations, out_grads, residue, warm_start.T]
+    held = [pltpu.VMEM(array.shape, array.dtype) for array in arrays[:3]]
+    return pl.pallas_call(
+        left_kernel,
+        in_specs=[pl.BlockSpec(memory_space=pltpu.HBM)] * 4,
+        out_specs=[WHOLE] * 4,
+        out_shape=[pltpu.VMEM((RANK, rows), jnp.float32), *held],
+        scratch_shapes=[
+            pltpu.VMEM((RANK, cols), warm_start.dtype),
+            pltpu.SemaphoreType.DMA((3 + GRAD_BLOCKS,)),
         ],
-        out_specs=pl.BlockSpec((2, rows, block), lambda i: (0, 0, i)),
-        out_shape=jax.ShapeDtypeStruct((2, rows, cols), jnp.bfloat16),
-        scratch_shapes=[pltpu.VMEM((rows, tokens), jnp.bfloat16)],
-        compiler_params=params(60),
-        cost_estimate=cost(2 * tokens * cols * rows, 2 * cols * (tokens + 3 * rows)),
-    )(activations, out_grads, residue)
-
-
-def right_kernel(left_ref, *refs):
-    *terms_refs, kept_ref, sent_ref = refs
-    cols = sum(terms_ref.shape[2] for terms_ref in terms_refs)
+        compiler_params=params(16),
+        cost_estimate=cost(2 * tokens * cols * RANK, 2 * cols * (tokens + rows)),
+    )(*[pltpu.with_memory_space_constraint(array, pltpu.HBM) for array in arrays])
+
+
+def right_kernel(left_ref, act_ref, grad_ref, res_ref, kept_ref, sent_ref):
+    cols = grad_ref.shape[1]
     peers, pair, _ = kept_ref.shape
     left = left_ref[...]
     swapped = jnp.concatenate([left[HALF:], left[:HALF]], axis=0)
-    high, low = kernel_split(jnp.where(lax.axis_index("core") == 0, left, swapped), 2)
-    stacked = jnp.concatenate([high, low], axis=0)
-    block = terms_refs[0].shape[2] // 2
-    for i in range(cols // block):
-        terms_ref, place = terms_refs[i // 2], slice(i % 2 * block, (i % 2 + 1) * block)
-        both = dot32(stacked, terms_ref[0, :, place])
-        product = both[:RANK] + (both[RANK:] + dot32(high, terms_ref[1, :, place]))
-        place = slice(i * block, (i + 1) * block)
+    ordered = kernel_split(jnp.where(lax.axis_index("core") == 0, left, swapped), 2)
+    ordered = jnp.concatenate(ordered, axis=0)
+    inner = dot32(ordered, act_ref[...], last_dims)
+    inner = jnp.concatenate(kernel_split(inner[:RANK] + inner[RANK:], 2), axis=0)
+    block = 512
+    for start in range(0, cols, block):
+        place = slice(start, start + block)
+        terms = dot32(inner, grad_ref[:, place]) + dot32(ordered, res_ref[:, place])
+        product = terms[:RANK] + terms[RANK:]
         kept_ref[:, :, place] = product[:HALF].reshape(peers, pair, block)
         sent_ref[:, :, place] = product[HALF:].reshape(peers, pair, block)
 
@@ -137,18 +143,18 @@
         sent_ref[:, :, place] = piece
 
 
-def right_product(left, terms):
-    rows, cols = left.shape[1], sum(part.shape[2] for part in terms)
+def right_product(left, activations, out_grads, residue):
+    (rows, cols), tokens = residue.shape, out_grads.shape[0]
     peers = peers_of(NEAR_X)
     shape = (peers, HALF // peers, cols + LANES * GRID["x"])
     return pl.pallas_call(
         right_kernel,
-        in_specs=[WHOLE] * (1 + len(terms)),
+        in_specs=[WHOLE] * 4,
         out_specs=[WHOLE] * 2,
         out_shape=[jax.ShapeDtypeStruct(shape, jnp.float32)] * 2,
         compiler_params=params(16),
-        cost_estimate=cost(6 * rows * cols * RANK, 4 * cols * rows),
-    )(left, *terms)
+        cost_estimate=cost(4 * (tokens + rows) * cols * RANK, 2 * cols * (tokens + rows)),
+    )(left, activations, out_grads, residue)
 
 
 def whiten_kernel(gram_ref, left_ref, out_ref):
@@ -262,17 +268,14 @@
 def local(activations, out_grads, residue, warm_start):
     residue = residue[0]
     rows, cols = residue.shape
-    core = lax.axis_index("core")
-    left = left_product(activations, out_grads, residue, warm_start)
-    left, activations, is_first = after(left, activations, core == 0)
-    terms_a = merged_terms(activations, out_grads, residue, 0)
-    left = exchange(left.reshape(peers_of(Z), -1, rows), Z)
-    left, terms_a, activations = after(sum_copies(left, Y, rows), terms_a, activations)
-    terms_b = merged_terms(activations, out_grads, residue, 1)
-    left, terms_b = after(sum_copies(exchange(left, Y), Z, rows), terms_b)
+    is_first = lax.axis_index("core") == 0
+    left, *held = left_product(activations, out_grads, residue, warm_start)
+    left, is_first = after(left, is_first)
+    left = sum_copies(exchange(left.reshape(peers_of(Z), -1, rows), Z), Y, rows)
+    left = sum_copies(exchange(left, Y), Z, rows)
     left = exchange(left, Z).reshape(RANK, rows)
 
-    kept, sent = right_product(left, [terms_a, terms_b])
+    kept, sent = right_product(left, *held)
     sent = lax.all_gather(sent, "core", axis=0)
     chunks = exchange(kept + jnp.where(is_first, sent[1], sent[0]), NEAR_X)
     scaled = whiten(chunks, left)

time: 110 us -> 105 us (0.955)
  blocking collectives: 45.8 us -> 77.4 us
  starting transfers between devices: 21.5 us -> 3.54 us
  matrix products: 6.09 us -> 0 us
  waiting for transfers between devices: 14 us -> 8.48 us
  Pallas kernels: 19.6 us -> 14.9 us
  local copies, waits for them, and re-layouts: 2.53 us -> 0 us
    all_to_all x3 -> x5, blocking collectives: 34.2 us -> 65.5 us  [exchange(): return lax.all_to_all(chunks, axes, 0, 0)]
    all_to_all x3 -> x1, starting transfers between devices: 21.5 us -> 3.54 us  [exchange(): return lax.all_to_all(chunks, axes, 0, 0)]
    dot_general x3 -> x0, matrix products: 6.09 us -> none  [dot32(): lax.dot_general(left, right, dims, preferred_element_type=jnp.float32)]
    all_to_all x3 -> x1, waiting for transfers between devices: 14 us -> 8.48 us  [exchange(): return lax.all_to_all(chunks, axes, 0, 0)]
    pallas_call x3 -> x2, Pallas kernels: 10.5 us -> 6.37 us  [the longest x1 4.74 us: left_product(): pl.pallas_call(left_kernel, in_specs=[pl.BlockSpec(memory_space=pltpu.HBM...]
    unnamed x10 -> x0, local copies, waits for them, and re-layouts: 2.53 us -> none
  transfers between devices with their start and end apart: 3 -> 1, of which waited for: 3 -> 1; matrix products, arithmetic and copies ran while one was open for 0% -> 0% of each run, Pallas kernels for 14% -> 6%
where the time goes in v4:
time: 105 us
  blocking collectives  77.4 us (74%)
  Pallas kernels  14.9 us (14%)
  waiting for transfers between devices  8.48 us (8%)
  starting transfers between devices  3.54 us (3%)
    all_to_all x5, blocking collectives, exchange(): return lax.all_to_all(chunks, axes, 0, 0)  65.5 us
    all_to_all x1, waiting for transfers between devices, exchange(): return lax.all_to_all(chunks, axes, 0, 0)  8.48 us
    all_gather x1, blocking collectives, local(): sent = lax.all_gather(sent, 'core', axis=0)  6.65 us
    pallas_call x1, Pallas kernels, whiten(): pl.pallas_call(whiten_kernel, grid=(1,), in_specs=[pl.BlockSpec((*chunks....  6.04 us
    all_gather x1, blocking collectives, local(): right = lax.all_gather(exchange(right, NEAR_X), 'core', axis=0)  5.33 us
    pallas_call x1, Pallas kernels, left_product(): pl.pallas_call(left_kernel, in_specs=[pl.BlockSpec(memory_space=pltpu.HBM...  4.74 us
    all_to_all x1, starting transfers between devices, exchange(): return lax.all_to_all(chunks, axes, 0, 0)  3.54 us
  transfers between devices with their start and end apart: 1, of which 1 were waited for; matrix products, arithmetic and copies ran while one was open for 0% of the time, Pallas kernels for 6%

profile of v4, /device:TPU:1, one launch (start us, length us, event | category | flops | bytes accessed | tf_op | source)
XLA Modules:
  0.0 104.6 jit_solution(10035714887578713006)
XLA Ops:
  0.0 4.7 %shard_map.46 = (f32[64,384]{1,0:T(8,128)S(1)}, bf16[1024,384]{1,0:T(8,128)(2,1)S(1)}, bf16[1024,2560]{1,0:T(8,128)(2,1)S(1)}, bf16[384,2560]{1,0:T(8,128)(2,1)S(1)}) custom-call(bf16[1024,384]{1,0:T(8,128)(2,1)} %act_hbm.1, bf16[1024,2560]{1,0:T(8,128)(2,1)} %grad_hbm.1, bf16[384,2560]{1,0:T(8,128)(2,1)} %bitcast.9, bf16[64,2560]{1,0:T(8,128)(2,1)} %bitcast.10), custom_call_target="tpu_custom_call" | custom-call | flops 335544320 | bytes 7208960 | tf_op jit(solution)/shard_map/pallas_call | solution.py:100
  4.8 18.3 %all_to_all.30.chunks_ref = f32[8,8,384]{2,1,0:T(8,128)S(1)} all-to-all(f32[8,8,384]{2,1,0:T(8,128)S(1)} %bitcast.8), channel_id=1, replica_groups=mesh['yA'=2,'yB'=2,'yC'=2,'zA'=2,'zB'=2,'zC'=2,'x'=4,'core'=2] {'zA','zB..., dimensions={0} | all-to-all | bytes 196608 | tf_op jit(solution)/shard_map/all_to_all | solution.py:261
  23.1 14.2 %all_to_all.31.chunks_ref = f32[8,8,384]{2,1,0:T(8,128)S(1)} all-to-all(f32[8,8,384]{2,1,0:T(8,128)S(1)} %shard_map.47), channel_id=1, replica_groups=mesh['yA'=2,'yB'=2,'yC'=2,'zA'=2,'zB'=2,'zC'=2,'x'=4,'core'=2] {'yA','yB..., dimensions={0} | all-to-all | bytes 196608 | tf_op jit(solution)/shard_map/all_to_all | solution.py:261
  37.3 10.0 %all_to_all.32 = f32[8,8,384]{2,1,0:T(8,128)S(1)} all-to-all(f32[8,8,384]{2,1,0:T(8,128)S(1)} %shard_map.48), channel_id=1, replica_groups=mesh['yA'=2,'yB'=2,'yC'=2,'zA'=2,'zB'=2,'zC'=2,'x'=4,'core'=2] {'zA','zB..., dimensions={0} | all-to-all | bytes 196608 | tf_op jit(solution)/shard_map/all_to_all | solution.py:261
  47.2 1.6 %shard_map.49 = (f32[16,2,3072]{2,1,0:T(2,128)S(1)}, f32[16,2,3072]{2,1,0:T(2,128)S(1)}) custom-call(f32[64,384]{1,0:T(8,128)S(1)} %bitcast.6, bf16[1024,384]{1,0:T(8,128)(2,1)S(1)} %get-tuple-element.17.act_ref, bf16[1024,2560]{1,0:T(8,128)(2,1)S(1)} %get-tuple-element.18.grad_ref, bf16[384,2560]{1,0:T(8,128)(2,1)S(1)} %get-tuple-element.19.res_ref), custom_call_target="tpu_custom_call" | custom-call | flops 922746880 | bytes 7208960 | tf_op jit(solution)/shard_map/pallas_call | solution.py:150
  48.9 6.6 %all-gather = f32[32,2,3072]{2,1,0:T(2,128)S(1)} all-gather(f32[16,2,3072]{2,1,0:T(2,128)S(1)} %get-tuple-element.22), channel_id=2, replica_groups=mesh['yA'=2,'yB'=2,'yC'=2,'zA'=2,'zB'=2,'zC'=2,'x'=4,'core'=2] {'core'}, dimensions={0}, use_global_device_ids=true | all-gather | bytes 1179648 | tf_op jit(solution)/shard_map/all_gather | solution.py:279
  55.5 0.3 fusion
  55.8 12.8 %all_to_all.33.chunks_ref.gram_ref = f32[16,2,3072]{2,1,0:T(2,128)S(1)} all-to-all(f32[16,2,3072]{2,1,0:T(2,128)S(1)} %fusion), channel_id=1, replica_groups=mesh['yA'=2,'yB'=2,'yC'=2,'zA'=2,'zB'=2,'zC'=2,'x'=4,'core'=2] {'yC','zC..., dimensions={0} | all-to-all | bytes 786432 | tf_op jit(solution)/shard_map/all_to_all | solution.py:261
  68.6 0.8 shard_map.50
  69.4 3.5 %all-to-all-start.4 = ((f32[16,2,2560]{2,1,0:T(2,128)}), f32[16,2,2560]{2,1,0:T(2,128)S(1)}, u32[]{:S(2)}, u32[]{:S(2)}) async-start(f32[16,2,2560]{2,1,0:T(2,128)} %shard_map.50), calls=%async_computation.4 | async-start | bytes 655360 | tf_op jit(solution)/shard_map/all_to_all | solution.py:261
  72.9 6.0 %shard_map.52.scaled_ref = bf16[384,192]{1,0:T(8,128)(2,1)S(1)} custom-call(f32[16,2,3072]{2,1,0:T(2,128)S(1)} %all_to_all.33.chunks_ref.gram_ref, f32[64,384]{1,0:T(8,128)S(1)} %bitcast.7), custom_call_target="tpu_custom_call" | custom-call | flops 400000000 | bytes 4000000 | tf_op jit(solution)/shard_map/pallas_call | solution.py:193
  79.0 8.5 %all-to-all-done.4.chunks_ref = f32[16,2,2560]{2,1,0:T(2,128)S(1)} async-done(((f32[16,2,2560]{2,1,0:T(2,128)}), f32[16,2,2560]{2,1,0:T(2,128)S(1)}, u32[]{:S(2)}, u32[]{:S(2)}) %all-to-all-start.4) | async-done | bytes 327712 | tf_op jit(solution)/shard_map/all_to_all | solution.py:261
  87.5 10.2 %all_to_all.34 = f32[16,2,2560]{2,1,0:T(2,128)S(1)} all-to-all(f32[16,2,2560]{2,1,0:T(2,128)S(1)} %shard_map.51), channel_id=1, replica_groups=mesh['yA'=2,'yB'=2,'yC'=2,'zA'=2,'zB'=2,'zC'=2,'x'=4,'core'=2] {'yC','zC..., dimensions={0} | all-to-all | bytes 655360 | tf_op jit(solution)/shard_map/all_to_all | solution.py:261
  97.7 5.3 %all-gather.1 = f32[32,2,2560]{2,1,0:T(2,128)S(1)} all-gather(f32[16,2,2560]{2,1,0:T(2,128)S(1)} %all_to_all.34), channel_id=3, replica_groups=mesh['yA'=2,'yB'=2,'yC'=2,'zA'=2,'zB'=2,'zC'=2,'x'=4,'core'=2] {'core'}, dimensions={0}, use_global_device_ids=true | all-gather | bytes 983040 | tf_op jit(solution)/shard_map/all_gather | solution.py:284
  103.0 1.6 %shard_map.53 = bf16[384,2560]{1,0:T(8,128)(2,1)} custom-call(bf16[384,192]{1,0:T(8,128)(2,1)S(1)} %shard_map.52.scaled_ref, f32[2,16,2,2560]{3,2,1,0:T(2,128)S(1)} %bitcast.5), custom_call_target="tpu_custom_call" | custom-call | flops 377487360 | bytes 1966080 | tf_op jit(solution)/shard_map/pallas_call | solution.py:224
  (3 shorter events, 0.1 us)
Async XLA Ops:
  69.4 18.1 %all-to-all-start.4 = ((f32[16,2,2560]{2,1,0:T(2,128)}), f32[16,2,2560]{2,1,0:T(2,128)S(1)}, u32[]{:S(2)}, u32[]{:S(2)}) async-start(f32[16,2,2560]{2,1,0:T(2,128)} %shard_map.50), calls=%async_computation.4 | async-start | bytes 655360 | tf_op jit(solution)/shard_map/all_to_all | solution.py:261

commit v5 on v4

--- a/solution.py
+++ b/solution.py
@@ -11,13 +11,14 @@
 HALF = RANK // 2
 LANES = 2 * RANK
 GRAD_BLOCKS = 2
-GRID = {"yA": 2, "yB": 2, "yC": 2, "zA": 2, "zB": 2, "zC": 2, "x": 4, "core": 2}
+GRID = {"yA": 2, "yB": 2, "yC": 2, "zA": 2, "zB": 2, "zC": 2, "xA": 2, "xB": 2, "core": 2}
 DP = ("yA", "yB", "yC", "zA", "zB", "zC")
-TENSOR = ("x", "core")
-Y, Z = DP[:3], DP[3:]
-NEAR = ("yC", "zC")
-NEAR_X = ("yC", "zC", "x")
-FAR = ("yA", "yB", "zA", "zB")
+TENSOR = ("xA", "xB", "core")
+LEFT_NEAR, LEFT_FAR = ("zC", "zB", "zA"), ("yC", "yB", "yA")
+NEAR = ("zC", "yC")
+X = ("xB", "xA")
+NEAR_X = (*X, "zC", "yC")
+FAR = ("zB", "zA", "yA", "yB")
 
 highest_precision = lax.Precision.HIGHEST
 plain_dims = (((1,), (0,)), ((), ()))
@@ -146,7 +147,7 @@
 def right_product(left, activations, out_grads, residue):
     (rows, cols), tokens = residue.shape, out_grads.shape[0]
     peers = peers_of(NEAR_X)
-    shape = (peers, HALF // peers, cols + LANES * GRID["x"])
+    shape = (peers, HALF // peers, cols + LANES * peers_of(X))
     return pl.pallas_call(
         right_kernel,
         in_specs=[WHOLE] * 4,
@@ -158,15 +159,14 @@
 
 
 def whiten_kernel(gram_ref, left_ref, out_ref):
-    shares, sources, pair = peers_of(NEAR), GRID["x"], gram_ref.shape[1]
+    shares, sources, pair = peers_of(NEAR), peers_of(X), gram_ref.shape[1]
     pieces = []
     for share in range(shares):
         for i in range(HALF // shares // pair):
             place = slice(i * LANES, (i + 1) * LANES)
-            first = share * sources
-            piece = gram_ref[first, :, place]
+            piece = gram_ref[share, :, place]
             for source in range(1, sources):
-                piece = piece + gram_ref[first + source, :, place]
+                piece = piece + gram_ref[source * shares + share, :, place]
             pieces.append(piece)
     gram = jnp.concatenate(pieces, axis=0)
     gram = jnp.concatenate([gram[:, :RANK], gram[:, RANK:]], axis=0)
@@ -188,7 +188,7 @@
 
 def whiten(chunks, left):
     rows = left.shape[1]
-    width = LANES * GRID["x"]
+    width = LANES * peers_of(X)
     last = chunks.shape[2] // width - 1
     return pl.pallas_call(
         whiten_kernel,
@@ -271,9 +271,9 @@
     is_first = lax.axis_index("core") == 0
     left, *held = left_product(activations, out_grads, residue, warm_start)
     left, is_first = after(left, is_first)
-    left = sum_copies(exchange(left.reshape(peers_of(Z), -1, rows), Z), Y, rows)
-    left = sum_copies(exchange(left, Y), Z, rows)
-    left = exchange(left, Z).reshape(RANK, rows)
+    left = sum_copies(exchange(left.reshape(peers_of(LEFT_NEAR), -1, rows), LEFT_NEAR), LEFT_FAR, rows)
+    left = sum_copies(exchange(left, LEFT_FAR), LEFT_NEAR, rows)
+    left = exchange(left, LEFT_NEAR).reshape(RANK, rows)
 
     kept, sent = right_product(left, *held)
     sent = lax.all_gather(sent, "core", axis=0)

time: 105 us -> 103 us (0.981)
  blocking collectives: 77.4 us -> 75 us
    all_to_all x5, blocking collectives: 65.5 us -> 64 us  [exchange(): return lax.all_to_all(chunks, axes, 0, 0)]
where the time goes in v5:
time: 103 us
  blocking collectives  75 us (73%)
  Pallas kernels  14.9 us (14%)
  waiting for transfers between devices  7.9 us (8%)
  starting transfers between devices  4.57 us (4%)
    all_to_all x5, blocking collectives, exchange(): return lax.all_to_all(chunks, axes, 0, 0)  64 us
    all_to_all x1, waiting for transfers between devices, exchange(): return lax.all_to_all(chunks, axes, 0, 0)  7.9 us
    all_gather x1, blocking collectives, local(): sent = lax.all_gather(sent, 'core', axis=0)  6.57 us
    pallas_call x1, Pallas kernels, whiten(): pl.pallas_call(whiten_kernel, grid=(1,), in_specs=[pl.BlockSpec((*chunks....  6.04 us
    pallas_call x1, Pallas kernels, left_product(): pl.pallas_call(left_kernel, in_specs=[pl.BlockSpec(memory_space=pltpu.HBM...  4.74 us
    all_to_all x1, starting transfers between devices, exchange(): return lax.all_to_all(chunks, axes, 0, 0)  4.57 us
    all_gather x1, blocking collectives, local(): right = lax.all_gather(exchange(right, NEAR_X), 'core', axis=0)  4.42 us
  transfers between devices with their start and end apart: 1, of which 1 were waited for; matrix products, arithmetic and copies ran while one was open for 0% of the time, Pallas kernels for 6%

profile of v5, /device:TPU:1, one launch (start us, length us, event | category | flops | bytes accessed | tf_op | source)
XLA Modules:
  0.0 102.7 jit_solution(3837682152128264940)
XLA Ops:
  0.0 4.7 %shard_map.46 = (f32[64,384]{1,0:T(8,128)S(1)}, bf16[1024,384]{1,0:T(8,128)(2,1)S(1)}, bf16[1024,2560]{1,0:T(8,128)(2,1)S(1)}, bf16[384,2560]{1,0:T(8,128)(2,1)S(1)}) custom-call(bf16[1024,384]{1,0:T(8,128)(2,1)} %act_hbm.1, bf16[1024,2560]{1,0:T(8,128)(2,1)} %grad_hbm.1, bf16[384,2560]{1,0:T(8,128)(2,1)} %bitcast.9, bf16[64,2560]{1,0:T(8,128)(2,1)} %bitcast.10), custom_call_target="tpu_custom_call" | custom-call | flops 335544320 | bytes 7208960 | tf_op jit(solution)/shard_map/pallas_call | solution.py:101
  4.8 17.4 %all_to_all.30.chunks_ref = f32[8,8,384]{2,1,0:T(8,128)S(1)} all-to-all(f32[8,8,384]{2,1,0:T(8,128)S(1)} %bitcast.8), channel_id=1, replica_groups=mesh['yA'=2,'yB'=2,'yC'=2,'zA'=2,'zB'=2,'zC'=2,'xA'=2,'xB'=2,'core'=2] {..., dimensions={0} | all-to-all | bytes 196608 | tf_op jit(solution)/shard_map/all_to_all | solution.py:261
  22.2 13.3 %all_to_all.31.chunks_ref = f32[8,8,384]{2,1,0:T(8,128)S(1)} all-to-all(f32[8,8,384]{2,1,0:T(8,128)S(1)} %shard_map.47), channel_id=1, replica_groups=mesh['yA'=2,'yB'=2,'yC'=2,'zA'=2,'zB'=2,'zC'=2,'xA'=2,'xB'=2,'core'=2] {..., dimensions={0} | all-to-all | bytes 196608 | tf_op jit(solution)/shard_map/all_to_all | solution.py:261
  35.5 9.2 %all_to_all.32 = f32[8,8,384]{2,1,0:T(8,128)S(1)} all-to-all(f32[8,8,384]{2,1,0:T(8,128)S(1)} %shard_map.48), channel_id=1, replica_groups=mesh['yA'=2,'yB'=2,'yC'=2,'zA'=2,'zB'=2,'zC'=2,'xA'=2,'xB'=2,'core'=2] {..., dimensions={0} | all-to-all | bytes 196608 | tf_op jit(solution)/shard_map/all_to_all | solution.py:261
  44.7 1.6 %shard_map.49 = (f32[16,2,3072]{2,1,0:T(2,128)S(1)}, f32[16,2,3072]{2,1,0:T(2,128)S(1)}) custom-call(f32[64,384]{1,0:T(8,128)S(1)} %bitcast.6, bf16[1024,384]{1,0:T(8,128)(2,1)S(1)} %get-tuple-element.17.act_ref, bf16[1024,2560]{1,0:T(8,128)(2,1)S(1)} %get-tuple-element.18.grad_ref, bf16[384,2560]{1,0:T(8,128)(2,1)S(1)} %get-tuple-element.19.res_ref), custom_call_target="tpu_custom_call" | custom-call | flops 922746880 | bytes 7208960 | tf_op jit(solution)/shard_map/pallas_call | solution.py:151
  46.4 6.6 %all-gather = f32[32,2,3072]{2,1,0:T(2,128)S(1)} all-gather(f32[16,2,3072]{2,1,0:T(2,128)S(1)} %get-tuple-element.22), channel_id=2, replica_groups=mesh['yA'=2,'yB'=2,'yC'=2,'zA'=2,'zB'=2,'zC'=2,'xA'=2,'xB'=2,'core'=2] {..., dimensions={0}, use_global_device_ids=true | all-gather | bytes 1179648 | tf_op jit(solution)/shard_map/all_gather | solution.py:279
  52.9 0.3 fusion
  53.2 12.2 %all_to_all.33.chunks_ref.gram_ref = f32[16,2,3072]{2,1,0:T(2,128)S(1)} all-to-all(f32[16,2,3072]{2,1,0:T(2,128)S(1)} %fusion), channel_id=1, replica_groups=mesh['yA'=2,'yB'=2,'yC'=2,'zA'=2,'zB'=2,'zC'=2,'xA'=2,'xB'=2,'core'=2] {..., dimensions={0} | all-to-all | bytes 786432 | tf_op jit(solution)/shard_map/all_to_all | solution.py:261
  65.4 0.8 shard_map.50
  66.2 4.6 %all-to-all-start.4 = ((f32[16,2,2560]{2,1,0:T(2,128)}), f32[16,2,2560]{2,1,0:T(2,128)S(1)}, u32[]{:S(2)}, u32[]{:S(2)}) async-start(f32[16,2,2560]{2,1,0:T(2,128)} %shard_map.50), calls=%async_computation.4 | async-start | bytes 655360 | tf_op jit(solution)/shard_map/all_to_all | solution.py:261
  70.8 6.0 %shard_map.52.scaled_ref = bf16[384,192]{1,0:T(8,128)(2,1)S(1)} custom-call(f32[16,2,3072]{2,1,0:T(2,128)S(1)} %all_to_all.33.chunks_ref.gram_ref, f32[64,384]{1,0:T(8,128)S(1)} %bitcast.7), custom_call_target="tpu_custom_call" | custom-call | flops 400000000 | bytes 4000000 | tf_op jit(solution)/shard_map/pallas_call | solution.py:193
  76.8 7.9 %all-to-all-done.4.chunks_ref = f32[16,2,2560]{2,1,0:T(2,128)S(1)} async-done(((f32[16,2,2560]{2,1,0:T(2,128)}), f32[16,2,2560]{2,1,0:T(2,128)S(1)}, u32[]{:S(2)}, u32[]{:S(2)}) %all-to-all-start.4) | async-done | bytes 327712 | tf_op jit(solution)/shard_map/all_to_all | solution.py:261
  84.8 11.9 %all_to_all.34 = f32[16,2,2560]{2,1,0:T(2,128)S(1)} all-to-all(f32[16,2,2560]{2,1,0:T(2,128)S(1)} %shard_map.51), channel_id=1, replica_groups=mesh['yA'=2,'yB'=2,'yC'=2,'zA'=2,'zB'=2,'zC'=2,'xA'=2,'xB'=2,'core'=2] {..., dimensions={0} | all-to-all | bytes 655360 | tf_op jit(solution)/shard_map/all_to_all | solution.py:261
  96.6 4.4 %all-gather.1 = f32[32,2,2560]{2,1,0:T(2,128)S(1)} all-gather(f32[16,2,2560]{2,1,0:T(2,128)S(1)} %all_to_all.34), channel_id=3, replica_groups=mesh['yA'=2,'yB'=2,'yC'=2,'zA'=2,'zB'=2,'zC'=2,'xA'=2,'xB'=2,'core'=2] {..., dimensions={0}, use_global_device_ids=true | all-gather | bytes 983040 | tf_op jit(solution)/shard_map/all_gather | solution.py:284
  101.0 1.6 %shard_map.53 = bf16[384,2560]{1,0:T(8,128)(2,1)} custom-call(bf16[384,192]{1,0:T(8,128)(2,1)S(1)} %shard_map.52.scaled_ref, f32[2,16,2,2560]{3,2,1,0:T(2,128)S(1)} %bitcast.5), custom_call_target="tpu_custom_call" | custom-call | flops 377487360 | bytes 1966080 | tf_op jit(solution)/shard_map/pallas_call | solution.py:224
  (3 shorter events, 0.1 us)
Async XLA Ops:
  66.2 18.5 %all-to-all-start.4 = ((f32[16,2,2560]{2,1,0:T(2,128)}), f32[16,2,2560]{2,1,0:T(2,128)S(1)}, u32[]{:S(2)}, u32[]{:S(2)}) async-start(f32[16,2,2560]{2,1,0:T(2,128)} %shard_map.50), calls=%async_computation.4 | async-start | bytes 655360 | tf_op jit(solution)/shard_map/all_to_all | solution.py:261

commit v6 on v5

--- a/solution.py
+++ b/solution.py
@@ -174,14 +174,20 @@
     col = lax.broadcasted_iota(jnp.int32, (RANK, RANK), 1)
     work = jnp.concatenate([gram, (row == col).astype(jnp.float32)], axis=1)
     tall = lax.broadcasted_iota(jnp.int32, (RANK, 2 * RANK), 0)
-    for k in range(RANK - 1):
-        pivot = work[k : k + 1, :]
-        scale = work[:, k : k + 1] / pivot[:, k : k + 1]
-        work = jnp.where(tall > k, work - scale * pivot, work)
-    inverse = work[:, RANK:]
-    diagonal = jnp.sum(jnp.where(row == col, work[:, :RANK], 0.0), axis=1, keepdims=True)
-    basis = dot_exact(inverse, left_ref[...])
-    scaled = dot_exact(basis, inverse / diagonal, first_dims)
+    weighted = []
+    for k in range(0, RANK, 2):
+        first, second = work[k : k + 1, :], work[k + 1 : k + 2, :]
+        corner, beside = 1.0 / first[:, k : k + 1], first[:, k + 1 : k + 2]
+        ratio = beside * corner
+        rest = 1.0 / (second[:, k + 1 : k + 2] - ratio * beside)
+        second = (second - ratio * first) * rest
+        first = (first - beside * second) * corner
+        weighted += [first[:, RANK:], second[:, RANK:]]
+        if k + 2 < RANK:
+            step = work[:, k : k + 1] * first + work[:, k + 1 : k + 2] * second
+            work = jnp.where(tall > k + 1, work - step, work)
+    basis = dot_exact(work[:, RANK:], left_ref[...])
+    scaled = dot_exact(basis, jnp.concatenate(weighted, axis=0), first_dims)
     high, low = kernel_split(scaled, 2)
     out_ref[...] = jnp.concatenate([high, high, low], axis=1)
 
@@ -278,9 +284,9 @@
     kept, sent = right_product(left, *held)
     sent = lax.all_gather(sent, "core", axis=0)
     chunks = exchange(kept + jnp.where(is_first, sent[1], sent[0]), NEAR_X)
+    right = exchange(sum_copies(chunks, FAR, cols), FAR)
+    right, chunks = after(sum_copies(right, NEAR_X, cols), chunks)
     scaled = whiten(chunks, left)
-    right = exchange(sum_copies(chunks, FAR, cols), FAR)
-    right, scaled = after(sum_copies(right, NEAR_X, cols), scaled)
     right = lax.all_gather(exchange(right, NEAR_X), "core", axis=0)
     return update_product(scaled, right)
 

time: 103 us -> 103 us (level)
  waiting for transfers between devices: 7.9 us -> 0.71 us
  blocking collectives: 75 us -> 81.6 us
    all_to_all x1, waiting for transfers between devices: 7.9 us -> 0.71 us  [exchange(): return lax.all_to_all(chunks, axes, 0, 0)]
    all_to_all x5, blocking collectives: 64 us -> 70.5 us  [exchange(): return lax.all_to_all(chunks, axes, 0, 0)]
where the time goes in v6:
time: 103 us
  blocking collectives  81.6 us (79%)
  Pallas kernels  15 us (15%)
  starting transfers between devices  5.02 us (5%)
    all_to_all x5, blocking collectives, exchange(): return lax.all_to_all(chunks, axes, 0, 0)  70.5 us
    all_gather x1, blocking collectives, local(): sent = lax.all_gather(sent, 'core', axis=0)  6.57 us
    pallas_call x1, Pallas kernels, whiten(): pl.pallas_call(whiten_kernel, grid=(1,), in_specs=[pl.BlockSpec((*chunks....  6.22 us
    all_to_all x1, starting transfers between devices, exchange(): return lax.all_to_all(chunks, axes, 0, 0)  5.02 us
    pallas_call x1, Pallas kernels, left_product(): pl.pallas_call(left_kernel, in_specs=[pl.BlockSpec(memory_space=pltpu.HBM...  4.74 us
    all_gather x1, blocking collectives, local(): right = lax.all_gather(exchange(right, NEAR_X), 'core', axis=0)  4.57 us
  transfers between devices with their start and end apart: 1, of which 1 were waited for; matrix products, arithmetic and copies ran while one was open for 0% of the time, Pallas kernels for 6%

profile of v6, /device:TPU:1, one launch (start us, length us, event | category | flops | bytes accessed | tf_op | source)
XLA Modules:
  0.0 102.7 jit_solution(3411227213069398824)
XLA Ops:
  0.0 4.7 %shard_map.46 = (f32[64,384]{1,0:T(8,128)S(1)}, bf16[1024,384]{1,0:T(8,128)(2,1)S(1)}, bf16[1024,2560]{1,0:T(8,128)(2,1)S(1)}, bf16[384,2560]{1,0:T(8,128)(2,1)S(1)}) custom-call(bf16[1024,384]{1,0:T(8,128)(2,1)} %act_hbm.1, bf16[1024,2560]{1,0:T(8,128)(2,1)} %grad_hbm.1, bf16[384,2560]{1,0:T(8,128)(2,1)} %bitcast.9, bf16[64,2560]{1,0:T(8,128)(2,1)} %bitcast.10), custom_call_target="tpu_custom_call" | custom-call | flops 335544320 | bytes 7208960 | tf_op jit(solution)/shard_map/pallas_call | solution.py:101
  4.8 17.4 %all_to_all.30.chunks_ref = f32[8,8,384]{2,1,0:T(8,128)S(1)} all-to-all(f32[8,8,384]{2,1,0:T(8,128)S(1)} %bitcast.8), channel_id=1, replica_groups=mesh['yA'=2,'yB'=2,'yC'=2,'zA'=2,'zB'=2,'zC'=2,'xA'=2,'xB'=2,'core'=2] {..., dimensions={0} | all-to-all | bytes 196608 | tf_op jit(solution)/shard_map/all_to_all | solution.py:267
  22.2 13.3 %all_to_all.31.chunks_ref = f32[8,8,384]{2,1,0:T(8,128)S(1)} all-to-all(f32[8,8,384]{2,1,0:T(8,128)S(1)} %shard_map.47), channel_id=1, replica_groups=mesh['yA'=2,'yB'=2,'yC'=2,'zA'=2,'zB'=2,'zC'=2,'xA'=2,'xB'=2,'core'=2] {..., dimensions={0} | all-to-all | bytes 196608 | tf_op jit(solution)/shard_map/all_to_all | solution.py:267
  35.5 9.2 %all_to_all.32 = f32[8,8,384]{2,1,0:T(8,128)S(1)} all-to-all(f32[8,8,384]{2,1,0:T(8,128)S(1)} %shard_map.48), channel_id=1, replica_groups=mesh['yA'=2,'yB'=2,'yC'=2,'zA'=2,'zB'=2,'zC'=2,'xA'=2,'xB'=2,'core'=2] {..., dimensions={0} | all-to-all | bytes 196608 | tf_op jit(solution)/shard_map/all_to_all | solution.py:267
  44.7 1.6 %shard_map.49 = (f32[16,2,3072]{2,1,0:T(2,128)S(1)}, f32[16,2,3072]{2,1,0:T(2,128)S(1)}) custom-call(f32[64,384]{1,0:T(8,128)S(1)} %bitcast.6, bf16[1024,384]{1,0:T(8,128)(2,1)S(1)} %get-tuple-element.17.act_ref, bf16[1024,2560]{1,0:T(8,128)(2,1)S(1)} %get-tuple-element.18.grad_ref, bf16[384,2560]{1,0:T(8,128)(2,1)S(1)} %get-tuple-element.19.res_ref), custom_call_target="tpu_custom_call" | custom-call | flops 922746880 | bytes 7208960 | tf_op jit(solution)/shard_map/pallas_call | solution.py:151
  46.4 6.6 %all-gather = f32[32,2,3072]{2,1,0:T(2,128)S(1)} all-gather(f32[16,2,3072]{2,1,0:T(2,128)S(1)} %get-tuple-element.22), channel_id=2, replica_groups=mesh['yA'=2,'yB'=2,'yC'=2,'zA'=2,'zB'=2,'zC'=2,'xA'=2,'xB'=2,'core'=2] {..., dimensions={0}, use_global_device_ids=true | all-gather | bytes 1179648 | tf_op jit(solution)/shard_map/all_gather | solution.py:285
  52.9 0.3 fusion
  53.2 12.2 %all_to_all.33.chunks_ref.gram_ref = f32[16,2,3072]{2,1,0:T(2,128)S(1)} all-to-all(f32[16,2,3072]{2,1,0:T(2,128)S(1)} %fusion), channel_id=1, replica_groups=mesh['yA'=2,'yB'=2,'yC'=2,'zA'=2,'zB'=2,'zC'=2,'xA'=2,'xB'=2,'core'=2] {..., dimensions={0} | all-to-all | bytes 786432 | tf_op jit(solution)/shard_map/all_to_all | solution.py:267
  65.5 18.3 %all_to_all.34.chunks_ref = f32[16,2,2560]{2,1,0:T(2,128)S(1)} all-to-all(f32[16,2,2560]{2,1,0:T(2,128)S(1)} %shard_map.50), channel_id=1, replica_groups=mesh['yA'=2,'yB'=2,'yC'=2,'zA'=2,'zB'=2,'zC'=2,'xA'=2,'xB'=2,'core'=2] {..., dimensions={0} | all-to-all | bytes 655360 | tf_op jit(solution)/shard_map/all_to_all | solution.py:267
  83.8 0.8 shard_map.51
  84.6 5.0 %all-to-all-start.5 = ((f32[16,2,2560]{2,1,0:T(2,128)}), f32[16,2,2560]{2,1,0:T(2,128)S(1)}, u32[]{:S(2)}, u32[]{:S(2)}) async-start(f32[16,2,2560]{2,1,0:T(2,128)} %shard_map.51), calls=%async_computation.5 | async-start | bytes 655360 | tf_op jit(solution)/shard_map/all_to_all | solution.py:267
  89.6 6.2 %shard_map.52.scaled_ref = bf16[384,192]{1,0:T(8,128)(2,1)S(1)} custom-call(f32[16,2,3072]{2,1,0:T(2,128)S(1)} %all_to_all.33.chunks_ref.gram_ref, f32[64,384]{1,0:T(8,128)S(1)} %bitcast.7), custom_call_target="tpu_custom_call" | custom-call | flops 400000000 | bytes 4000000 | tf_op jit(solution)/shard_map/pallas_call | solution.py:199
  95.8 0.7 all-to-all-done.5
  96.5 4.6 %all-gather.1 = f32[32,2,2560]{2,1,0:T(2,128)S(1)} all-gather(f32[16,2,2560]{2,1,0:T(2,128)S(1)} %all-to-all-done.5), channel_id=3, replica_groups=mesh['yA'=2,'yB'=2,'yC'=2,'zA'=2,'zB'=2,'zC'=2,'xA'=2,'xB'=2,'core'=2] {..., dimensions={0}, use_global_device_ids=true | all-gather | bytes 983040 | tf_op jit(solution)/shard_map/all_gather | solution.py:290
  101.1 1.6 %shard_map.53 = bf16[384,2560]{1,0:T(8,128)(2,1)} custom-call(bf16[384,192]{1,0:T(8,128)(2,1)S(1)} %shard_map.52.scaled_ref, f32[2,16,2,2560]{3,2,1,0:T(2,128)S(1)} %bitcast.5), custom_call_target="tpu_custom_call" | custom-call | flops 377487360 | bytes 1966080 | tf_op jit(solution)/shard_map/pallas_call | solution.py:230
  (3 shorter events, 0.1 us)
Async XLA Ops:
  84.6 12.0 %all-to-all-start.5 = ((f32[16,2,2560]{2,1,0:T(2,128)}), f32[16,2,2560]{2,1,0:T(2,128)S(1)}, u32[]{:S(2)}, u32[]{:S(2)}) async-start(f32[16,2,2560]{2,1,0:T(2,128)} %shard_map.51), calls=%async_computation.5 | async-start | bytes 655360 | tf_op jit(solution)/shard_map/all_to_all | solution.py:267

commit v7 on v5

--- a/solution.py
+++ b/solution.py
@@ -14,11 +14,11 @@
 GRID = {"yA": 2, "yB": 2, "yC": 2, "zA": 2, "zB": 2, "zC": 2, "xA": 2, "xB": 2, "core": 2}
 DP = ("yA", "yB", "yC", "zA", "zB", "zC")
 TENSOR = ("xA", "xB", "core")
-LEFT_NEAR, LEFT_FAR = ("zC", "zB", "zA"), ("yC", "yB", "yA")
+LEFT_NEAR, LEFT_FAR = ("zB", "zC", "zA"), ("yB", "yC", "yA")
 NEAR = ("zC", "yC")
 X = ("xB", "xA")
 NEAR_X = (*X, "zC", "yC")
-FAR = ("zB", "zA", "yA", "yB")
+FAR = ("yB", "yA", "zA", "zB")
 
 highest_precision = lax.Precision.HIGHEST
 plain_dims = (((1,), (0,)), ((), ()))
@@ -278,9 +278,9 @@
     kept, sent = right_product(left, *held)
     sent = lax.all_gather(sent, "core", axis=0)
     chunks = exchange(kept + jnp.where(is_first, sent[1], sent[0]), NEAR_X)
+    right = exchange(sum_copies(chunks, FAR, cols), FAR)
+    right, chunks = after(sum_copies(right, NEAR_X, cols), chunks)
     scaled = whiten(chunks, left)
-    right = exchange(sum_copies(chunks, FAR, cols), FAR)
-    right, scaled = after(sum_copies(right, NEAR_X, cols), scaled)
     right = lax.all_gather(exchange(right, NEAR_X), "core", axis=0)
     return update_product(scaled, right)
 

time: 103 us -> 103 us (level)
  blocking collectives: 75 us -> 82.6 us
  waiting for transfers between devices: 7.9 us -> 0.87 us
    all_to_all x1, waiting for transfers between devices: 7.9 us -> 0.87 us  [exchange(): return lax.all_to_all(chunks, axes, 0, 0)]
    all_to_all x5, blocking collectives: 64 us -> 69.4 us  [exchange(): return lax.all_to_all(chunks, axes, 0, 0)]
    all_gather x1, blocking collectives: 4.42 us -> 6.41 us  [local(): right = lax.all_gather(exchange(right, NEAR_X), 'core', axis=0)]
where the time goes in v7:
time: 103 us
  blocking collectives  82.6 us (80%)
  Pallas kernels  14.9 us (14%)
  starting transfers between devices  4.22 us (4%)
    all_to_all x5, blocking collectives, exchange(): return lax.all_to_all(chunks, axes, 0, 0)  69.4 us
    all_gather x1, blocking collectives, local(): sent = lax.all_gather(sent, 'core', axis=0)  6.79 us
    all_gather x1, blocking collectives, local(): right = lax.all_gather(exchange(right, NEAR_X), 'core', axis=0)  6.41 us
    pallas_call x1, Pallas kernels, whiten(): pl.pallas_call(whiten_kernel, grid=(1,), in_specs=[pl.BlockSpec((*chunks....  6.04 us
    pallas_call x1, Pallas kernels, left_product(): pl.pallas_call(left_kernel, in_specs=[pl.BlockSpec(memory_space=pltpu.HBM...  4.74 us
    all_to_all x1, starting transfers between devices, exchange(): return lax.all_to_all(chunks, axes, 0, 0)  4.22 us
  transfers between devices with their start and end apart: 1, of which 1 were waited for; matrix products, arithmetic and copies ran while one was open for 0% of the time, Pallas kernels for 6%

profile of v7, /device:TPU:1, one launch (start us, length us, event | category | flops | bytes accessed | tf_op | source)
XLA Modules:
  0.0 102.9 jit_solution(8029757110779702307)
XLA Ops:
  0.0 4.7 %shard_map.46 = (f32[64,384]{1,0:T(8,128)S(1)}, bf16[1024,384]{1,0:T(8,128)(2,1)S(1)}, bf16[1024,2560]{1,0:T(8,128)(2,1)S(1)}, bf16[384,2560]{1,0:T(8,128)(2,1)S(1)}) custom-call(bf16[1024,384]{1,0:T(8,128)(2,1)} %act_hbm.1, bf16[1024,2560]{1,0:T(8,128)(2,1)} %grad_hbm.1, bf16[384,2560]{1,0:T(8,128)(2,1)} %bitcast.9, bf16[64,2560]{1,0:T(8,128)(2,1)} %bitcast.10), custom_call_target="tpu_custom_call" | custom-call | flops 335544320 | bytes 7208960 | tf_op jit(solution)/shard_map/pallas_call | solution.py:101
  4.8 17.4 %all_to_all.30.chunks_ref = f32[8,8,384]{2,1,0:T(8,128)S(1)} all-to-all(f32[8,8,384]{2,1,0:T(8,128)S(1)} %bitcast.8), channel_id=1, replica_groups=mesh['yA'=2,'yB'=2,'yC'=2,'zA'=2,'zB'=2,'zC'=2,'xA'=2,'xB'=2,'core'=2] {..., dimensions={0} | all-to-all | bytes 196608 | tf_op jit(solution)/shard_map/all_to_all | solution.py:261
  22.2 13.4 %all_to_all.31.chunks_ref = f32[8,8,384]{2,1,0:T(8,128)S(1)} all-to-all(f32[8,8,384]{2,1,0:T(8,128)S(1)} %shard_map.47), channel_id=1, replica_groups=mesh['yA'=2,'yB'=2,'yC'=2,'zA'=2,'zB'=2,'zC'=2,'xA'=2,'xB'=2,'core'=2] {..., dimensions={0} | all-to-all | bytes 196608 | tf_op jit(solution)/shard_map/all_to_all | solution.py:261
  35.6 9.1 %all_to_all.32 = f32[8,8,384]{2,1,0:T(8,128)S(1)} all-to-all(f32[8,8,384]{2,1,0:T(8,128)S(1)} %shard_map.48), channel_id=1, replica_groups=mesh['yA'=2,'yB'=2,'yC'=2,'zA'=2,'zB'=2,'zC'=2,'xA'=2,'xB'=2,'core'=2] {..., dimensions={0} | all-to-all | bytes 196608 | tf_op jit(solution)/shard_map/all_to_all | solution.py:261
  44.7 1.6 %shard_map.49 = (f32[16,2,3072]{2,1,0:T(2,128)S(1)}, f32[16,2,3072]{2,1,0:T(2,128)S(1)}) custom-call(f32[64,384]{1,0:T(8,128)S(1)} %bitcast.6, bf16[1024,384]{1,0:T(8,128)(2,1)S(1)} %get-tuple-element.17.act_ref, bf16[1024,2560]{1,0:T(8,128)(2,1)S(1)} %get-tuple-element.18.grad_ref, bf16[384,2560]{1,0:T(8,128)(2,1)S(1)} %get-tuple-element.19.res_ref), custom_call_target="tpu_custom_call" | custom-call | flops 922746880 | bytes 7208960 | tf_op jit(solution)/shard_map/pallas_call | solution.py:151
  46.4 6.8 %all-gather = f32[32,2,3072]{2,1,0:T(2,128)S(1)} all-gather(f32[16,2,3072]{2,1,0:T(2,128)S(1)} %get-tuple-element.22), channel_id=2, replica_groups=mesh['yA'=2,'yB'=2,'yC'=2,'zA'=2,'zB'=2,'zC'=2,'xA'=2,'xB'=2,'core'=2] {..., dimensions={0}, use_global_device_ids=true | all-gather | bytes 1179648 | tf_op jit(solution)/shard_map/all_gather | solution.py:279
  53.1 0.3 fusion
  53.4 12.9 %all_to_all.33.chunks_ref.gram_ref = f32[16,2,3072]{2,1,0:T(2,128)S(1)} all-to-all(f32[16,2,3072]{2,1,0:T(2,128)S(1)} %fusion), channel_id=1, replica_groups=mesh['yA'=2,'yB'=2,'yC'=2,'zA'=2,'zB'=2,'zC'=2,'xA'=2,'xB'=2,'core'=2] {..., dimensions={0} | all-to-all | bytes 786432 | tf_op jit(solution)/shard_map/all_to_all | solution.py:261
  66.3 16.6 %all_to_all.34.chunks_ref = f32[16,2,2560]{2,1,0:T(2,128)S(1)} all-to-all(f32[16,2,2560]{2,1,0:T(2,128)S(1)} %shard_map.50), channel_id=1, replica_groups=mesh['yA'=2,'yB'=2,'yC'=2,'zA'=2,'zB'=2,'zC'=2,'xA'=2,'xB'=2,'core'=2] {..., dimensions={0} | all-to-all | bytes 655360 | tf_op jit(solution)/shard_map/all_to_all | solution.py:261
  82.9 0.8 shard_map.51
  83.7 4.2 %all-to-all-start.5 = ((f32[16,2,2560]{2,1,0:T(2,128)}), f32[16,2,2560]{2,1,0:T(2,128)S(1)}, u32[]{:S(2)}, u32[]{:S(2)}) async-start(f32[16,2,2560]{2,1,0:T(2,128)} %shard_map.51), calls=%async_computation.5 | async-start | bytes 655360 | tf_op jit(solution)/shard_map/all_to_all | solution.py:261
  87.9 6.0 %shard_map.52.scaled_ref = bf16[384,192]{1,0:T(8,128)(2,1)S(1)} custom-call(f32[16,2,3072]{2,1,0:T(2,128)S(1)} %all_to_all.33.chunks_ref.gram_ref, f32[64,384]{1,0:T(8,128)S(1)} %bitcast.7), custom_call_target="tpu_custom_call" | custom-call | flops 400000000 | bytes 4000000 | tf_op jit(solution)/shard_map/pallas_call | solution.py:193
  94.0 0.9 all-to-all-done.5
  94.9 6.4 %all-gather.1 = f32[32,2,2560]{2,1,0:T(2,128)S(1)} all-gather(f32[16,2,2560]{2,1,0:T(2,128)S(1)} %all-to-all-done.5), channel_id=3, replica_groups=mesh['yA'=2,'yB'=2,'yC'=2,'zA'=2,'zB'=2,'zC'=2,'xA'=2,'xB'=2,'core'=2] {..., dimensions={0}, use_global_device_ids=true | all-gather | bytes 983040 | tf_op jit(solution)/shard_map/all_gather | solution.py:284
  101.3 1.6 %shard_map.53 = bf16[384,2560]{1,0:T(8,128)(2,1)} custom-call(bf16[384,192]{1,0:T(8,128)(2,1)S(1)} %shard_map.52.scaled_ref, f32[2,16,2,2560]{3,2,1,0:T(2,128)S(1)} %bitcast.5), custom_call_target="tpu_custom_call" | custom-call | flops 377487360 | bytes 1966080 | tf_op jit(solution)/shard_map/pallas_call | solution.py:224
  (3 shorter events, 0.1 us)
Async XLA Ops:
  83.7 11.1 %all-to-all-start.5 = ((f32[16,2,2560]{2,1,0:T(2,128)}), f32[16,2,2560]{2,1,0:T(2,128)S(1)}, u32[]{:S(2)}, u32[]{:S(2)}) async-start(f32[16,2,2560]{2,1,0:T(2,128)} %shard_map.51), calls=%async_computation.5 | async-start | bytes 655360 | tf_op jit(solution)/shard_map/all_to_all | solution.py:261
